TPU v7x, 512 devices: a whole 4x4x16 slice. The times are simulated.
512 devices in a mesh: user: 64 (over z, x), item: 4 (over y), rep: 2 (over core).
Axes of the slice: x: 4, y: 4, z: 16, core: 2. Of those that a mesh axis runs over, the one named last changes fastest.
Arguments:
- user_factors: bfloat16 [16384, 256], P('user'), may hold values from -6 to 6
- item_factors: bfloat16 [196608, 256], P(('user', 'item')), may hold values from -6 to 6
- item_bucket: int32 [196608], P(('user', 'item')), may hold values from 0 to 15
- propensity: float32 [16], replicated, may hold values from 0.02 to 1
- tile_blocks: int32 [128, 128], P('user', 'item'), may hold values from 0 to 1535, as said below
- positives: int32 [16384, 128], P('user', 'item'), may hold values from -64 to 127
Outputs:
- new_users: bfloat16 [16384, 256], P('user')
- new_items: bfloat16 [196608, 256], P(('user', 'item'))
Inputs may be any that keep to these rules, and one draw needn't show every extreme that they name: `tile_blocks`: column q * 2 * 16 + r * 16 + k (k below 16) of a row names an item block g with (g // 6) % 4 == q. The 32 blocks of one row and one q are distinct and have distinct values of g // 24. Over the 2 rows of one user shard (rows s * 2 to s * 2 + 1) and one q, at most one block of each value of g // 24 is named, and for each q some such value is named in every user shard.
All inputs are finite; a program needn't handle non-finite values.
Results may differ from a plain program's by a relative error of at most 0.015.
Values may be sent and summed in bfloat16 or wider, within the bound.
A program may use at most 64 MiB of HBM per device.

v0:
```python
import jax
import jax.numpy as jnp
from jax import lax
from jax.sharding import PartitionSpec as P

BLK = 128


STEP_USER = 0.02
STEP_ITEM = 0.1
DECAY = 0.1


def body(user_factors, item_factors, item_bucket, propensity, tile_blocks, positives):
    user_count = lax.axis_size("user")
    rep_count = lax.axis_size("rep")
    rep_index = lax.axis_index("rep")
    rank_width = user_factors.shape[1]
    score_scale = rank_width ** (-0.5)
    blocks_here = item_factors.shape[0] // BLK
    spread = lax.axis_size("item") * blocks_here
    slot_count = tile_blocks.shape[1] // rep_count
    own_tiles = lax.dynamic_slice_in_dim(tile_blocks, rep_index * slot_count, slot_count, 1)
    own_pos = lax.dynamic_slice_in_dim(positives, rep_index * slot_count, slot_count, 1)
    owner_ids = own_tiles // spread
    peer_index = jnp.arange(user_count, dtype=jnp.int32)
    item_stack = item_factors.reshape(blocks_here, BLK, rank_width)
    bucket_stack = item_bucket.reshape(blocks_here, BLK)
    flat_tiles = own_tiles.reshape(-1)
    match = (flat_tiles // spread)[:, None] == peer_index[None, :]
    wanted_block = jnp.max(jnp.where(match, (flat_tiles % blocks_here)[:, None], -1), axis=0)
    asked_block = lax.all_to_all(
        wanted_block.reshape(user_count, 1), "user", split_axis=0, concat_axis=0, tiled=True
    ).reshape(user_count)
    picked = jnp.maximum(asked_block, 0)
    sent_buckets = bucket_stack[picked]
    fetched, got_buckets = (
        lax.all_to_all(item_stack[picked], "user", split_axis=0, concat_axis=0, tiled=True),
        lax.all_to_all(sent_buckets, "user", split_axis=0, concat_axis=0, tiled=True),
    )
    inverse_table = 1.0 / propensity
    bucket_match = (
        got_buckets[:, :, None] == jnp.arange(propensity.shape[0], dtype=jnp.int32)[None, None, :]
    )
    inverse_fetched = jnp.sum(jnp.where(bucket_match, inverse_table[None, None, :], 0.0), axis=-1)
    columns = jnp.arange(BLK, dtype=jnp.int32)

    def tile_terms(user_block, owners, pos_rows):
        item_tiles = fetched[owners]
        inverse_prop = inverse_fetched[owners]
        raw_scores = jnp.einsum(
            "ar,kjr->kaj", user_block, item_tiles, preferred_element_type=jnp.float32
        )
        is_positive = pos_rows.T[:, :, None] == columns[None, None, :]
        target_sign = jnp.where(is_positive, 1.0, -1.0).astype(jnp.float32)
        weight = jnp.where(is_positive, inverse_prop[:, None, :], 1.0)
        margin = jnp.maximum(1.0 - target_sign * raw_scores * score_scale, 0.0)
        hinge_grad = (-2.0 * score_scale * target_sign * weight * margin).astype(jnp.bfloat16)
        return (hinge_grad, item_tiles)

    pos_blocks = own_pos.reshape(-1, BLK, slot_count)

    def first_pass(carry, inputs):
        user_block, owners, pos_rows = inputs
        hinge_grad, item_tiles = tile_terms(user_block, owners, pos_rows)
        return (
            carry,
            jnp.einsum("kaj,kjr->ar", hinge_grad, item_tiles, preferred_element_type=jnp.float32),
        )

    unused, user_partial = lax.scan(
        first_pass,
        jnp.zeros((), jnp.float32),
        (user_factors.reshape(-1, BLK, rank_width), owner_ids, pos_blocks),
    )
    user_partial = user_partial.reshape(-1, rank_width)
    old_users = user_factors.astype(jnp.float32)
    grad_total = lax.psum(user_partial, ("item", "rep"))
    new_users = (old_users - STEP_USER * (grad_total + DECAY * old_users)).astype(jnp.bfloat16)

    def second_pass(panels, inputs):
        user_block, owners, pos_rows = inputs
        hinge_grad, item_tiles = tile_terms(user_block, owners, pos_rows)
        item_terms = jnp.einsum(
            "kaj,ar->kjr", hinge_grad, user_block, preferred_element_type=jnp.float32
        )
        return (panels.at[owners].add(item_terms), None)

    empty_panels = jnp.zeros((user_count, BLK, rank_width), jnp.float32)
    panels, unused_rows = lax.scan(
        second_pass, empty_panels, (new_users.reshape(-1, BLK, rank_width), owner_ids, pos_blocks)
    )
    old_items = item_factors.astype(jnp.float32)
    onehot = (asked_block[None, :] == jnp.arange(blocks_here, dtype=jnp.int32)[:, None]).astype(
        jnp.float32
    )
    returned = lax.all_to_all(
        panels.astype(jnp.bfloat16), "user", split_axis=0, concat_axis=0, tiled=True
    ).astype(panels.dtype)
    grad_local = jnp.dot(onehot, returned.reshape(user_count, -1), precision=lax.Precision.HIGHEST)
    grad_local = grad_local.reshape(blocks_here * BLK, rank_width)
    item_share = lax.psum_scatter(
        grad_local.astype(jnp.bfloat16), "rep", scatter_dimension=0, tiled=True
    ).astype(jnp.float32)
    share_rows = item_share.shape[0]
    own_items = lax.dynamic_slice_in_dim(old_items, rep_index * share_rows, share_rows, 0)
    new_rows = (own_items - STEP_ITEM * (item_share + DECAY * own_items)).astype(jnp.bfloat16)
    new_items = lax.all_gather(new_rows, "rep", axis=0, tiled=True)
    return (new_users, new_items)


def solution(mesh):
    return jax.shard_map(
        body,
        mesh=mesh,
        in_specs=(
            P("user", None),
            P(("user", "item"), None),
            P(("user", "item")),
            P(),
            P("user", "item"),
            P("user", "item"),
        ),
        out_specs=(P("user", None), P(("user", "item"), None)),
        check_vma=False,
    )
```

profile of v0, /device:TPU:1, one launch (start us, length us, event | category | flops | bytes accessed | tf_op | source)
XLA Modules:
  0.0 593.2 jit_solution(5912180581719886842)
XLA Ops:
  8.4 32.4 %all_to_all.28 = s32[64,1,1]{2,1,0:T(1,128)S(1)} all-to-all(s32[64,1,1]{2,1,0:T(1,128)S(1)} %copy.21), channel_id=1, replica_groups=mesh['user'=64,'item'=4,'rep'=2] {'user'}, dimensions={0} | all-to-all | bytes 512 | tf_op jit(solution)/shard_map/all_to_all | solution.py:32
  40.8 2.4 fusion.73
  43.1 1.9 gather_fusion.4
  45.0 4.6 all-to-all-start.1
  49.6 3.8 gather_fusion.5
  53.4 9.7 %all-to-all-done.1 = s32[64,1,128]{2,1,0:T(1,128)S(1)} async-done(((s32[64,1,128]{2,1,0:T(1,128)}), s32[64,1,128]{2,1,0:T(1,128)S(1)}, u32[]{:S(2)}, u32[]{:S(2)}) %all-to-all-start.1) | async-done | bytes 32800 | tf_op jit(solution)/shard_map/all_to_all | solution.py:39
  63.1 5.7 all-to-all-start.2
  69.1 182.5 %all-to-all-done.2 = bf16[64,128,256]{2,1,0:T(8,128)(2,1)} async-done(((bf16[64,128,256]{2,1,0:T(8,128)(2,1)}), bf16[64,128,256]{2,1,0:T(8,128)(2,1)}, u32[]{:S(2)}, u32[]{:S(2)}) %all-to-all-start.2) | async-done | bytes 4194336 | tf_op jit(solution)/shard_map/all_to_all | solution.py:38
  251.7 8.6 %while.22 = (s32[]{:T(128)}, f32[2,128,256]{2,1,0:T(8,128)S(1)}, s32[2,128,16]{1,2,0:T(8,128)S(1)}, s32[2,16]{1,0:T(2,128)S(1)}, f32[64,128]{1,0:T(8,128)S(1)}, ...) while((s32[]{:T(128)}, f32[2,128,256]{2,1,0:T(8,128)S(1)}, ...), condition=%wide.region_3.4_spmd.clone, body=%wide.region_2.3_spmd.clone.sunk | while | flops 271320128 | bytes 4445605 | solution.py:71
  252.3 2.8 gather_fusion
  256.6 2.8 gather_fusion
  261.1 73.0 %all-reduce.2.cloned.1.call-done = f32[256,256]{1,0:T(8,128)} async-done(((f32[256,256]{1,0:T(8,128)}), f32[256,256]{1,0:T(8,128)}) %all-reduce.2.cloned.1.call-update) | async-done | bytes 262160 | tf_op jit(solution)/shard_map/psum | solution.py:78
  335.1 4.2 broadcast_in_dim.89
  339.3 17.7 %while.23 = (s32[]{:T(128)}, f32[64,128,256]{2,1,0:T(8,128)}, s32[2,16]{1,0:T(2,128)S(1)}, s32[2,128,16]{1,2,0:T(8,128)S(1)}, f32[64,128]{1,0:T(8,128)S(1)}, /*i...) while((s32[]{:T(128)}, f32[64,128,256]{2,1,0:T(8,128)}, ...), condition=%wide.region_7.8_spmd.clone, body=%wide.region_5.7_spmd.clone.sunk | while | flops 271844416 | bytes 11720165 | solution.py:90
  339.9 2.8 gather_fusion.2
  343.6 4.6 scatter_fusion
  348.7 2.8 gather_fusion.2
  352.4 4.7 scatter_fusion
  357.0 4.0 convert_element_type.35
  361.1 198.6 %all_to_all.29 = bf16[64,128,256]{2,1,0:T(8,128)(2,1)S(1)} all-to-all(bf16[64,128,256]{2,1,0:T(8,128)(2,1)S(1)} %convert_element_type.35), channel_id=1, replica_groups=mesh['user'=64,'item'=4,'rep'=2] {'user'}, dimensions={0} | all-to-all | bytes 8388608 | tf_op jit(solution)/shard_map/all_to_all | solution.py:97
  559.7 2.6 copy.27
  562.9 1.4 convert_element_type.37
  564.3 18.2 %reduce-scatter.2.cloned.1.call-done = bf16[384,256]{1,0:T(8,128)(2,1)} async-done(((bf16[768,256]{1,0:T(8,128)(2,1)}), bf16[384,256]{1,0:T(8,128)(2,1)}) %reduce-scatter.2.cloned.1.call-update) | async-done | bytes 196624 | tf_op jit(solution)/shard_map/reduce_scatter | solution.py:102
  583.5 2.1 all_gather.3
  (52 shorter events, 11.5 us)
Async XLA Ops:
  7.2 61.7 %copy-start = (s32[256,32]{0,1:T(8,128)S(1)}, s32[256,32]{0,1:T(8,128)}, u32[]{:S(2)}) copy-start(s32[256,32]{0,1:T(8,128)} %param.15) | copy-start | bytes 98308
  45.0 18.1 %all-to-all-start.1 = ((s32[64,1,128]{2,1,0:T(1,128)}), s32[64,1,128]{2,1,0:T(1,128)S(1)}, u32[]{:S(2)}, u32[]{:S(2)}) async-start(s32[64,1,128]{2,1,0:T(1,128)} %bitcast.3), calls=%async_computation.1 | async-start | bytes 65536 | tf_op jit(solution)/shard_map/all_to_all | solution.py:39
  53.4 15.5 %copy-start.5 = (f32[16]{0:T(128)S(1)}, f32[16]{0:T(128)}, u32[]{:S(2)}) copy-start(f32[16]{0:T(128)} %param.13) | copy-start | bytes 196
  53.4 198.3 %copy-start.3 = (bf16[256,256]{1,0:T(8,128)(2,1)S(1)}, bf16[256,256]{1,0:T(8,128)(2,1)}, u32[]{:S(2)}) copy-start(bf16[256,256]{1,0:T(8,128)(2,1)} %param.10) | copy-start | bytes 393220
  63.1 188.5 %all-to-all-start.2 = ((bf16[64,128,256]{2,1,0:T(8,128)(2,1)}), bf16[64,128,256]{2,1,0:T(8,128)(2,1)}, u32[]{:S(2)}, u32[]{:S(2)}) async-start(bf16[64,128,256]{2,1,0:T(8,128)(2,1)} %gather_fusion.5), calls=%async_computation.2 | async-start | bytes 8388608 | tf_op jit(solution)/shard_map/all_to_all | solution.py:38
  68.8 265.3 %all-reduce.2.cloned.1.call-start = ((), (), s32[]{:S(2)}) async-start(), calls=%async_computation.5 | async-start | bytes 524288 | tf_op jit(solution)/shard_map/psum | solution.py:78
  260.3 0.7 copy-start.2
  261.0 321.5 %reduce-scatter.2.cloned.1.call-start = ((), (), s32[]{:S(2)}) async-start(), calls=%async_computation.6 | async-start | bytes 589824 | tf_op jit(solution)/shard_map/reduce_scatter | solution.py:102
  357.0 4.0 copy-start.4
  562.3 20.2 %copy-start.1 = (bf16[768,256]{1,0:T(8,128)(2,1)S(1)}, bf16[768,256]{1,0:T(8,128)(2,1)}, u32[]{:S(2)}) copy-start(bf16[768,256]{1,0:T(8,128)(2,1)} %param.11) | copy-start | bytes 1179652
Sparse Core Ops, SparseCore 0:
  261.2 72.8 all-reduce.1
  564.4 18.0 reduce-scatter.1
where the time goes:
time: 594 us; the launch traced here: 593 us
  waiting for transfers between devices  284 us (48%)
  blocking collectives  233 us (39%)
  local copies, waits for them, and re-layouts  29.2 us (5%)
  other arithmetic  18.8 us (3%)
  between operations  14.2 us (2%)
  starting transfers between devices  10.3 us (2%)
    all_to_all x1, blocking collectives, body(): lax.all_to_all(panels.astype(jnp.bfloat16), 'user', split_axis=0, concat_...  199 us
    all_to_all x1, waiting for transfers between devices, body(): lax.all_to_all(item_stack[picked], 'user', split_axis=0, concat_axis=0, t...  183 us
    psum x1, waiting for transfers between devices, body(): grad_total = lax.psum(user_partial, ('item', 'rep'))  73 us
    all_to_all x1, blocking collectives, body(): lax.all_to_all(wanted_block.reshape(user_count, 1), 'user', split_axis=0,...  32.4 us
    reduce_scatter x1, waiting for transfers between devices, body(): lax.psum_scatter(grad_local.astype(jnp.bfloat16), 'rep', scatter_dimensio...  18.2 us
  transfers between devices with their start and end apart: 4, of which 4 were waited for; matrix products, arithmetic and copies ran while one was open for 1% of the time, Pallas kernels for 0%

commit v1 on v0

v1 whole, which is shorter than its diff:
```python
import functools

import jax
import jax.numpy as jnp
from jax import lax
from jax.experimental import pallas as pl
from jax.experimental.pallas import tpu as pltpu
from jax.sharding import PartitionSpec as P

BLK = 128
STEP_USER = 0.02
STEP_ITEM = 0.1
DECAY = 0.1
MESH = pl.DeviceIdType.MESH
F32 = jnp.float32
BF16 = jnp.bfloat16

NX = 4
NY = 4
IBD = 6
RANK = 256
HB = IBD // 2
HALF = HB * BLK
QR = BLK // NY


def nt(a, b):
    return lax.dot_general(a, b, (((1,), (1,)), ((), ())), preferred_element_type=F32)


def nn(a, b):
    return lax.dot_general(a, b, (((1,), (0,)), ((), ())), preferred_element_type=F32)


def kernel(nz, u_ref, it_ref, bk_ref, prop_ref, tb_ref, pos_ref, ou_ref, oi_ref,
           cm, cr, idv, ids, items, invp, invrow, invcol, ua, ub, gs, yr, zs_buf, zr, hexp,
           cs, ccr, xs, xr, own_sum,
           c_s, c_r, sm_sem, i_s, i_r, f_s, f_r, p_s, p_r, az_s, az_r, ay_s, ay_r,
           ry_s, ry_r, rz_s, rz_r, bz_s, bz_r, by_s, by_r, g_s, g_r, x_s, x_r, o_s, o_r, l_sem):
    user = lax.axis_index("user")
    y = lax.axis_index("item")
    r = lax.axis_index("rep")
    z = user // NX
    x = user % NX
    c = RANK ** -0.5

    def zdev(zz):
        return (zz * NX + x, y, r)

    def xdev(xx):
        return (z * NX + xx, y, r)

    def ydev(yy):
        return (user, yy, r)

    sib = (user, y, 1 - r)

    def rc(src, dst, ss, rs, dev):
        return pltpu.make_async_remote_copy(
            src_ref=src, dst_ref=dst, send_sem=ss, recv_sem=rs, device_id=dev, device_id_type=MESH)

    def zpeer(i):
        return lax.rem(z + 7 * i, nz)

    def zsrc(i):
        return lax.rem(z + (nz - 7 % nz) * i, nz)

    def off(base, i, n):
        return lax.rem(base + i, n)

    barrier = pltpu.get_barrier_semaphore()

    def greet(i, carry):
        pl.semaphore_signal(barrier, inc=1, device_id=zdev(zpeer(i)), device_id_type=MESH)
        return carry

    lax.fori_loop(1, nz, greet, 0)
    for d in range(1, NX):
        pl.semaphore_signal(barrier, inc=1, device_id=xdev(off(x, d, NX)), device_id_type=MESH)
    for d in range(1, NY):
        pl.semaphore_signal(barrier, inc=1, device_id=ydev(off(y, d, NY)), device_id_type=MESH)
    pl.semaphore_signal(barrier, inc=1, device_id=sib, device_id_type=MESH)

    tb = tb_ref[pl.ds(r, 1), :]
    owner = (tb * 2731) >> 16
    local = tb - owner * (NY * IBD) - y * IBD
    ow_rows = lax.broadcasted_iota(jnp.int32, (nz * NX, tb.shape[1]), 0)
    hot = jnp.where(ow_rows == owner, 1.0, 0.0)
    pos = pos_ref[pl.ds(pl.multiple_of(r * BLK, BLK), BLK), :].astype(F32).astype(BF16)
    pos_by = nt(hot.astype(BF16), pos)
    named = jnp.sum(hot, axis=1, keepdims=True)
    pos_by = jnp.where(named > 0.0, pos_by, -1.0).astype(jnp.int32)
    z_rows = lax.broadcasted_iota(jnp.int32, (nz, tb.shape[1]), 0)
    id_lane = lax.broadcasted_iota(jnp.int32, (nz, BLK), 1)
    id_mat = jnp.zeros((nz, BLK), jnp.int32)
    for xx in range(NX):
        asked = jnp.max(jnp.where(owner == z_rows * NX + xx, local + 1, 0), axis=1, keepdims=True)
        id_mat = jnp.where(id_lane == xx, asked, id_mat)
    for zz in range(nz):
        cm[zz, 0:NX, :] = pos_by[zz * NX:(zz + 1) * NX, :]
        cm[zz, 8:9, :] = id_mat[zz:zz + 1, :]

    bk = bk_ref[...]
    inv = jnp.zeros((IBD, BLK), F32)
    for b in range(16):
        inv = inv + jnp.where(bk == b, 1.0 / jnp.full((IBD, BLK), prop_ref[0, b], F32), 0.0)
    invp[x, 0:IBD, :] = inv * (2.0 * c)

    cr[z] = cm[z]
    ua[z] = u_ref[pl.ds(pl.multiple_of(r * BLK, BLK), BLK), :]
    own_items = pltpu.make_async_copy(it_ref, items.at[x], l_sem)
    own_items.start()

    pl.semaphore_wait(barrier, nz - 1 + NX - 1 + NY - 1 + 1)

    q0 = pl.multiple_of(y * QR, QR)
    h0 = r * HB

    def code_copy(i):
        p = zpeer(i)
        return rc(cm.at[p], cr.at[z], c_s.at[p], c_r.at[z], zdev(p))

    def send_codes(i, carry):
        code_copy(i).start()
        return carry

    def item_copy(d):
        p = off(x, d, NX)
        return rc(it_ref.at[pl.ds(h0, HB)], items.at[x, pl.ds(h0, HB)], i_s.at[p], i_r.at[x], xdev(p))

    def invp_copy(d):
        p = off(x, d, NX)
        return rc(invp.at[x], invp.at[x], p_s.at[p], p_r.at[x], xdev(p))

    def az_copy(i):
        p = zpeer(i)
        return rc(ua.at[z, pl.ds(q0, QR)], ua.at[z, pl.ds(q0, QR)], az_s.at[p], az_r.at[z], zdev(p))

    def send_users(i, carry):
        az_copy(i).start()
        return carry

    for d in (2, 1, 3):
        item_copy(d).start()
    lax.fori_loop(1, nz, send_users, 0)
    lax.fori_loop(1, nz, send_codes, 0)
    for d in (2, 1, 3):
        invp_copy(d).start()

    def forward_y(buf, zz, ss, rs):
        for d in range(1, NY):
            rc(buf.at[zz, pl.ds(q0, QR)], buf.at[zz, pl.ds(q0, QR)], ss.at[zz], rs.at[zz], ydev(off(y, d, NY))).start()

    def three(buf, zz, ss, rs):
        part = buf.at[zz, pl.ds(0, QR * (NY - 1))]
        return rc(part, part, ss.at[zz], rs.at[zz], ydev(off(y, 1, NY)))

    def arrive_z(buf, zz, ss, rs):
        part = buf.at[zz, pl.ds(q0, QR)]
        rc(part, part, ss.at[zz], rs.at[zz], zdev(zz)).wait_recv()

    def forward_first(i, carry):
        zz = zsrc(i)
        arrive_z(ua, zz, az_s, az_r)
        forward_y(ua, zz, ay_s, ay_r)
        return carry

    lax.fori_loop(1, nz, forward_first, 0)

    def sib_items(xx):
        part = items.at[xx, pl.ds(h0, HB)]
        return rc(part, part, f_s.at[xx], f_r.at[xx], sib)

    def sib_items_in(xx):
        part = items.at[xx, pl.ds((1 - r) * HB, HB)]
        return rc(part, part, f_s.at[xx], f_r.at[xx], sib)

    for d in (3, 1, 2):
        xx = off(x, d, NX)
        part = items.at[xx, pl.ds(h0, HB)]
        rc(part, part, i_s.at[xx], i_r.at[xx], xdev(xx)).wait_recv()
        sib_items(xx).start()
    for d in (3, 1, 2):
        xx = off(x, d, NX)
        rc(invp.at[xx], invp.at[xx], p_s.at[xx], p_r.at[xx], xdev(xx)).wait_recv()

    def take_codes(i, carry):
        zz = zsrc(i)
        rc(cm.at[zz], cr.at[zz], c_s.at[zz], c_r.at[zz], zdev(zz)).wait_recv()
        return carry

    lax.fori_loop(1, nz, take_codes, 0)

    for zz in range(nz):
        idv[zz:zz + 1, :] = cr[zz, 8:9, :]
    to_smem = pltpu.make_async_copy(idv, ids, sm_sem)
    to_smem.start()

    for xx in range(NX):
        cols = jnp.transpose(invp[xx])
        for j in range(IBD):
            invcol[xx, j] = jnp.broadcast_to(cols[:, j:j + 1], (BLK, BLK))
            invrow[xx, j] = jnp.broadcast_to(invp[xx, j:j + 1, :], (8, BLK))

    to_smem.wait()
    own_items.wait()
    for d in (3, 1, 2):
        sib_items_in(off(x, d, NX)).wait_recv()

    lane = lax.broadcasted_iota(jnp.int32, (BLK, BLK), 1)
    lane_f = lane.astype(F32)
    sub = lax.broadcasted_iota(jnp.int32, (BLK, BLK), 0)

    def pick(zz, xx):
        code = ids[zz, xx]
        j = jnp.maximum(code - 1, 0)
        block = items[xx, j]
        flat = jnp.where(code > 0, 2.0 * c, 0.0).astype(F32)
        return code, j, block, flat

    def grads(zz):
        users = ua[zz]
        cols = jnp.transpose(cr[zz, 0:8, :].astype(F32))
        blocks, hs = [], []
        picks = [pick(zz, xx) for xx in range(NX)]
        stack = jnp.concatenate([p[2] for p in picks], axis=0)
        scores = nt(users, stack)
        for xx in range(NX):
            code, j, block, flat = picks[xx]
            s = scores[:, xx * BLK:(xx + 1) * BLK]
            hit = cols[:, xx:xx + 1] == lane_f
            w = invrow[xx, j][0:1, :]
            m = jnp.maximum(1.0 + s * jnp.where(hit, -c, c), 0.0)
            hs.append((m * jnp.where(hit, -w, flat)).astype(BF16))
        return nn(jnp.concatenate(hs, axis=1), stack)

    def ry_copy(zz, d):
        p = off(y, d, NY)
        return rc(gs.at[zz, pl.ds(pl.multiple_of(p * QR, QR), QR)], yr.at[zz, pl.ds(q0, QR)],
                  ry_s.at[zz], ry_r.at[zz], ydev(p))

    def first_pass(i, carry):
        zz = zsrc(i)

        @pl.when(i > 0)
        def _():
            three(ua, zz, ay_s, ay_r).wait_recv()

        gs[zz] = grads(zz).astype(BF16)
        for d in (2, 1, 3):
            ry_copy(zz, d).start()
        return carry

    lax.fori_loop(0, nz, first_pass, 0)

    def rz_copy(zz):
        return rc(zs_buf.at[zz], zr.at[z], rz_s.at[zz], rz_r.at[z], zdev(zz))

    def sum_y(zz):
        part = yr.at[zz, pl.ds(0, QR * (NY - 1))]
        rc(part, part, ry_s.at[zz], ry_r.at[zz], ydev(off(y, 1, NY))).wait_recv()
        total = gs[zz, pl.ds(q0, QR), :].astype(F32)
        for d in range(1, NY):
            total = total + yr[zz, pl.ds(pl.multiple_of(off(y, d, NY) * QR, QR), QR), :].astype(F32)
        return total

    own_sum[...] = sum_y(z)

    def second_sum(i, carry):
        zz = zsrc(i)
        zs_buf[zz] = sum_y(zz).astype(BF16)
        rz_copy(zz).start()
        return carry

    lax.fori_loop(1, nz, second_sum, 0)

    def gather_sum(i, carry):
        zz = zsrc(i)
        rc(zs_buf.at[zz], zr.at[zz], rz_s.at[zz], rz_r.at[zz], zdev(zz)).wait_recv()
        own_sum[...] += zr[zz].astype(F32)
        return carry

    lax.fori_loop(1, nz, gather_sum, 0)

    old = u_ref[pl.ds(pl.multiple_of(r * BLK + q0, QR), QR), :].astype(F32)
    ub[z, pl.ds(q0, QR), :] = (old - STEP_USER * (own_sum[...] + DECAY * old)).astype(BF16)

    def bz_copy(i):
        p = zpeer(i)
        return rc(ub.at[z, pl.ds(q0, QR)], ub.at[z, pl.ds(q0, QR)], bz_s.at[p], bz_r.at[z], zdev(p))

    def send_new(i, carry):
        bz_copy(i).start()
        return carry

    lax.fori_loop(1, nz, send_new, 0)
    forward_y(ub, z, by_s, by_r)

    def forward_second(i, carry):
        zz = zsrc(i)
        arrive_z(ub, zz, bz_s, bz_r)
        forward_y(ub, zz, by_s, by_r)
        return carry

    def expand(zz):
        users = ub[zz]
        z0 = pl.multiple_of(zz * BLK, BLK)
        for xx in range(NX):
            code, j, block, flat = pick(zz, xx)
            s = nt(block, users)
            hit = cr[zz, xx:xx + 1, :] == sub
            m = jnp.maximum(1.0 + s * jnp.where(hit, -c, c), 0.0)
            h = m * jnp.where(hit, -invcol[xx, j], flat)
            for jj in range(IBD):
                hexp[xx, jj * BLK:(jj + 1) * BLK, pl.ds(z0, BLK)] = jnp.where(code == jj + 1, h, 0.0).astype(BF16)

    LAG = 3

    def second_pass(i, carry):
        @pl.when(jnp.logical_and(i > 0, i < nz))
        def _():
            forward_second(i, 0)

        @pl.when(i >= LAG)
        def _():
            zz = zsrc(i - LAG)
            three(ub, zz, by_s, by_r).wait_recv()
            expand(zz)

        return carry

    lax.fori_loop(0, nz + LAG, second_pass, 0)

    b0 = pl.multiple_of(r * BLK, BLK)
    ou_ref[pl.ds(b0, BLK), :] = ub[z]
    out_u = rc(ub.at[z], ou_ref.at[pl.ds(b0, BLK)], o_s.at[0], o_r.at[0], sib)
    out_u.start()

    flat_users = ub.reshape(nz * BLK, RANK)

    def item_dot(xx, h):
        rows = hexp[xx, pl.ds(pl.multiple_of(h * HALF, HALF), HALF), :]
        return nn(rows, flat_users[...])

    def core_copy(xx):
        return rc(cs.at[xx], ccr.at[xx], g_s.at[xx], g_r.at[xx], sib)

    def other_half(k, carry):
        xx = lax.rem(x + k + 1, NX)
        cs[xx] = item_dot(xx, 1 - r).astype(BF16)
        core_copy(xx).start()
        return carry

    lax.fori_loop(0, NX, other_half, 0)

    def x_copy(xx):
        return rc(xs.at[xx], xr.at[x], x_s.at[xx], x_r.at[x], xdev(xx))

    def own_half(k, carry):
        xx = lax.rem(x + k + 1, NX)
        mine = item_dot(xx, r)
        core_copy(xx).wait_recv()
        xs[xx] = (mine + ccr[xx].astype(F32)).astype(BF16)

        @pl.when(k < NX - 1)
        def _():
            x_copy(xx).start()

        return carry

    lax.fori_loop(0, NX, own_half, 0)
    total = xs[x].astype(F32)
    for d in (1, 3, 2):
        xx = off(x, d, NX)
        rc(xs.at[xx], xr.at[xx], x_s.at[xx], x_r.at[xx], xdev(xx)).wait_recv()
        total = total + xr[xx].astype(F32)
    olds = it_ref[pl.ds(h0, HB)].astype(F32)
    total = total.reshape(HB, BLK, RANK)
    oi_ref[pl.ds(h0, HB)] = (olds - STEP_ITEM * (total + DECAY * olds)).astype(BF16)
    out_i = rc(oi_ref.at[pl.ds(h0, HB)], oi_ref.at[pl.ds(h0, HB)], o_s.at[1], o_r.at[1], sib)
    out_i.start()

    for d in (2, 1, 3):
        item_copy(d).wait_send()
        invp_copy(d).wait_send()
        xx = off(x, d, NX)
        sib_items(xx).wait_send()
        x_copy(xx).wait_send()
    for d in range(NX):
        core_copy(off(x, d, NX)).wait_send()

    def sent(i, carry):
        code_copy(i).wait_send()
        az_copy(i).wait_send()
        bz_copy(i).wait_send()
        zz = zsrc(i)
        three(ua, zz, ay_s, ay_r).wait_send()
        rz_copy(zz).wait_send()
        return carry

    lax.fori_loop(1, nz, sent, 0)

    def sent_all(i, carry):
        three(ub, i, by_s, by_r).wait_send()
        three(gs, i, ry_s, ry_r).wait_send()
        return carry

    lax.fori_loop(0, nz, sent_all, 0)
    out_u.wait_send()
    out_i.wait_send()
    other_b = pl.multiple_of((1 - r) * BLK, BLK)
    other_h = (1 - r) * HB
    rc(ub.at[z], ou_ref.at[pl.ds(other_b, BLK)], o_s.at[0], o_r.at[0], sib).wait_recv()
    rc(oi_ref.at[pl.ds(other_h, HB)], oi_ref.at[pl.ds(other_h, HB)], o_s.at[1], o_r.at[1], sib).wait_recv()


def body(nz, user_factors, item_factors, item_bucket, propensity, tile_blocks, positives):
    dma = pltpu.SemaphoreType.DMA
    V = pltpu.VMEM
    scratch = [
        V((nz, 16, BLK), jnp.int32),
        V((nz, 16, BLK), jnp.int32),
        V((nz, BLK), jnp.int32),
        pltpu.SMEM((nz, BLK), jnp.int32),
        V((NX, IBD, BLK, RANK), BF16),
        V((NX, 8, BLK), F32),
        V((NX, IBD, 8, BLK), F32),
        V((NX, IBD, BLK, BLK), F32),
        V((nz, BLK, RANK), BF16),
        V((nz, BLK, RANK), BF16),
        V((nz, BLK, RANK), BF16),
        V((nz, BLK, RANK), BF16),
        V((nz, QR, RANK), BF16),
        V((nz, QR, RANK), BF16),
        V((NX, IBD * BLK, nz * BLK), BF16),
        V((NX, HALF, RANK), BF16),
        V((NX, HALF, RANK), BF16),
        V((NX, HALF, RANK), BF16),
        V((NX, HALF, RANK), BF16),
        V((QR, RANK), F32),
        dma((nz,)), dma((nz,)), dma,
        dma((NX,)), dma((NX,)), dma((NX,)), dma((NX,)), dma((NX,)), dma((NX,)),
        dma((nz,)), dma((nz,)), dma((nz,)), dma((nz,)),
        dma((nz,)), dma((nz,)), dma((nz,)), dma((nz,)),
        dma((nz,)), dma((nz,)), dma((nz,)), dma((nz,)),
        dma((NX,)), dma((NX,)), dma((NX,)), dma((NX,)),
        dma((2,)), dma((2,)), dma,
    ]
    vmem = pl.BlockSpec(memory_space=pltpu.VMEM)
    new_users, new_items = pl.pallas_call(
        functools.partial(kernel, nz),
        out_shape=(
            jax.ShapeDtypeStruct(user_factors.shape, BF16),
            jax.ShapeDtypeStruct((IBD, BLK, RANK), BF16),
        ),
        in_specs=[vmem, vmem, vmem, pl.BlockSpec(memory_space=pltpu.SMEM), vmem, vmem],
        out_specs=(vmem, vmem),
        scratch_shapes=scratch,
        compiler_params=pltpu.CompilerParams(
            collective_id=0, has_side_effects=True, vmem_limit_bytes=56 << 20),
    )(
        user_factors,
        item_factors.reshape(IBD, BLK, RANK),
        item_bucket.reshape(IBD, BLK),
        propensity.reshape(1, -1),
        tile_blocks,
        positives,
    )
    return new_users, new_items.reshape(item_factors.shape)


def solution(mesh):
    nz = mesh.shape["user"] // NX
    return jax.shard_map(
        functools.partial(body, nz),
        mesh=mesh,
        in_specs=(
            P("user", None),
            P(("user", "item"), None),
            P(("user", "item")),
            P(),
            P("user", "item"),
            P("user", "item"),
        ),
        out_specs=(P("user", None), P(("user", "item"), None)),
        check_vma=False,
    )
```

time: 594 us -> 114 us (0.19)
  waiting for transfers between devices: 284 us -> 0 us
  blocking collectives: 233 us -> 0 us
  Pallas kernels: 0 us -> 108 us
  local copies, waits for them, and re-layouts: 29.2 us -> 4.85 us
  other arithmetic: 18.8 us -> 0 us
  between operations: 14.2 us -> 0.64 us
  starting transfers between devices: 10.3 us -> 0 us
    all_to_all x2 -> x0, blocking collectives: 231 us -> none  [the longest x1 199 us: body(): lax.all_to_all(panels.astype(jnp.bfloat16), 'user', split_axis=0, concat_...]
    all_to_all x2 -> x0, waiting for transfers between devices: 192 us -> none  [the longest x1 183 us: body(): lax.all_to_all(item_stack[picked], 'user', split_axis=0, concat_axis=0, t...]
    pallas_call x0 -> x1, Pallas kernels: none -> 108 us  [body(): pl.pallas_call(functools.partial(kernel, nz), out_shape=(jax.ShapeDtypeSt...]
    psum x1 -> x0, waiting for transfers between devices: 73 us -> none  [body(): grad_total = lax.psum(user_partial, ('item', 'rep'))]
    gather x10 -> x0, local copies, waits for them, and re-layouts: 19.1 us -> none  [the longest x4 11.2 us: tile_terms(): item_tiles = fetched[owners]]
    reduce_scatter x1 -> x0, waiting for transfers between devices: 18.2 us -> none  [body(): lax.psum_scatter(grad_local.astype(jnp.bfloat16), 'rep', scatter_dimensio...]
    all_to_all x2 -> x0, starting transfers between devices: 10.3 us -> none  [the longest x1 5.67 us: body(): lax.all_to_all(item_stack[picked], 'user', split_axis=0, concat_axis=0, t...]
    scatter-add x2 -> x0, other arithmetic: 9.23 us -> none  [second_pass(): return (panels.at[owners].add(item_terms), None)]
  transfers between devices with their start and end apart: 4 -> 0, of which waited for: 4 -> 0; matrix products, arithmetic and copies ran while one was open for 1% -> 0% of each run, Pallas kernels for 0% -> 0%
where the time goes in v1:
time: 114 us
  Pallas kernels  108 us (95%)
  local copies, waits for them, and re-layouts  4.85 us (4%)
    pallas_call x1, Pallas kernels, body(): pl.pallas_call(functools.partial(kernel, nz), out_shape=(jax.ShapeDtypeSt...  108 us
    unnamed x3, local copies, waits for them, and re-layouts  4.85 us

profile of v1, /device:TPU:1, one launch (start us, length us, event | category | flops | bytes accessed | tf_op | source)
XLA Modules:
  0.0 113.6 jit_solution(136790517177764935)
XLA Ops:
  0.6 1.5 %copy.8.pos_ref = s32[256,32]{1,0:T(8,128)} copy(s32[256,32]{0,1:T(8,128)} %param.11) | data formatting | bytes 65536 | tf_op args[5]
  2.1 108.2 %shard_map.77 = (bf16[256,256]{1,0:T(8,128)(2,1)}, bf16[6,128,256]{2,1,0:T(8,128)(2,1)}) custom-call(bf16[256,256]{1,0:T(8,128)(2,1)} %u_ref.1, bf16[6,128,256]{2,1,0:T(8,128)(2,1)} %bitcast.4, s32[6,128]{1,0:T(8,128)} %bitcast.6, f32[1,16]{1,0:T(1,128)} %bitcast.7, s32[2,32]{1,0:T(2,128)} %tb_ref.1, s32[256,32]{1,0:T(8,128)} %copy.8.pos_ref), custom_call_target="tpu_custom_call" | custom-call | tf_op jit(solution)/shard_map/pallas_call | solution.py:450
  110.3 1.6 %copy.11 = bf16[256,256]{1,0:T(8,128)(2,1)} copy(bf16[256,256]{1,0:T(8,128)(2,1)} %get-tuple-element.8) | data formatting | bytes 262144
  111.9 1.8 %copy.12 = bf16[768,256]{1,0:T(8,128)(2,1)} copy(bf16[768,256]{1,0:T(8,128)(2,1)} %bitcast.5) | data formatting | bytes 786432

commit v2 on v0

v2 whole, which is shorter than its diff:
```python
import functools

import jax
import jax.numpy as jnp
from jax import lax
from jax.experimental import pallas as pl
from jax.experimental.pallas import tpu as pltpu
from jax.sharding import PartitionSpec as P

BLK = 128
STEP_USER = 0.02
STEP_ITEM = 0.1
DECAY = 0.1
MESH = pl.DeviceIdType.MESH
F32 = jnp.float32
BF16 = jnp.bfloat16

NX = 4
NY = 4
IBD = 6
RANK = 256
HB = IBD // 2
HALF = HB * BLK
QR = BLK // NY
NO = 2 * NX
ZB = 2
ZB2 = 2
ZROWS = ZB2 * BLK
LAG1 = 4
LAG2 = 3


def nt(a, b):
    return lax.dot_general(a, b, (((1,), (1,)), ((), ())), preferred_element_type=F32)


def nn(a, b):
    return lax.dot_general(a, b, (((1,), (0,)), ((), ())), preferred_element_type=F32)


def kernel(na, u_ref, it_ref, bk_ref, prop_ref, tb_ref, pos_ref, ou_ref, oi_ref,
           cm, cr, idv, ids, items, invp, invrow, invcol, ua, ub, gs, yr, zs_buf, zr, hexp,
           cs, ccr, xs, zrec, xrec, xrec1, psum, prec, own_sum,
           c_s, c_r, sm_sem, ix_s, ix_r, iz_s, iz_r, jx_s, jx_r, jz_s, jz_r, f_s, f_r,
           p_s, p_r, pz_s, pz_r, pf_s, pf_r,
           az_s, az_r, ay_s, ay_r, ry_s, ry_r, rz_s, rz_r, bz_s, bz_r, by_s, by_r,
           g_s, g_r, x_s, x_r, w_s, w_r, v_s, v_r, t_s, t_r, o_s, o_r, l_sem):
    user = lax.axis_index("user")
    y = lax.axis_index("item")
    r = lax.axis_index("rep")
    z = user // NX
    x = user % NX
    m = z // 2
    p = z % 2
    own = NX * p
    far = NX - own
    k0 = own + x
    c = RANK ** -0.5

    def zdev(mm):
        return ((2 * mm + p) * NX + x, y, r)

    def xdev(xx):
        return (z * NX + xx, y, r)

    def ydev(yy):
        return (user, yy, r)

    sib = (user, y, 1 - r)
    mate = ((2 * m + 1 - p) * NX + x, y, r)

    def rc(src, dst, ss, rs, dev):
        return pltpu.make_async_remote_copy(
            src_ref=src, dst_ref=dst, send_sem=ss, recv_sem=rs, device_id=dev, device_id_type=MESH)

    def step(i):
        return na // 2 + (2 * (i % 2) - 1) * ((i + 1) // 2)

    def peer(i):
        return lax.rem(m + step(i), na)

    def source(i):
        return lax.rem(m + 2 * na - step(i), na)

    def off(base, i, n):
        return lax.rem(base + i, n)

    barrier = pltpu.get_barrier_semaphore()

    def greet(i, carry):
        pl.semaphore_signal(barrier, inc=1, device_id=zdev(peer(i)), device_id_type=MESH)
        return carry

    lax.fori_loop(0, na - 1, greet, 0)
    for d in range(1, NX):
        pl.semaphore_signal(barrier, inc=1, device_id=xdev(off(x, d, NX)), device_id_type=MESH)
    for d in range(1, NY):
        pl.semaphore_signal(barrier, inc=1, device_id=ydev(off(y, d, NY)), device_id_type=MESH)
    pl.semaphore_signal(barrier, inc=1, device_id=sib, device_id_type=MESH)
    pl.semaphore_signal(barrier, inc=1, device_id=mate, device_id_type=MESH)

    b0 = pl.multiple_of(r * BLK, BLK)
    q0 = pl.multiple_of(y * QR, QR)
    h0 = r * HB
    own_items = pltpu.make_async_copy(it_ref, items.at[k0], l_sem.at[0])
    own_items.start()
    own_users = pltpu.make_async_copy(u_ref.at[pl.ds(b0, BLK)], ua.at[m], l_sem.at[1])
    own_users.start()

    tb = tb_ref[pl.ds(r, 1), :]
    owner = (tb * 2731) >> 16
    local = tb - owner * (NY * IBD) - y * IBD
    ow_rows = lax.broadcasted_iota(jnp.int32, (na * NO, tb.shape[1]), 0)
    hot = jnp.where(ow_rows == owner, 1.0, 0.0)
    pos = pos_ref[:, pl.ds(b0, BLK)].astype(F32).astype(BF16)
    pos_by = nn(hot.astype(BF16), pos)
    named = jnp.sum(hot, axis=1, keepdims=True)
    pos_by = jnp.where(named > 0.0, pos_by, -1.0).astype(jnp.int32)
    m_rows = lax.broadcasted_iota(jnp.int32, (na, tb.shape[1]), 0)
    id_lane = lax.broadcasted_iota(jnp.int32, (na, BLK), 1)
    id_mat = jnp.zeros((na, BLK), jnp.int32)
    for k in range(NO):
        asked = jnp.max(jnp.where(owner == m_rows * NO + k, local + 1, 0), axis=1, keepdims=True)
        id_mat = jnp.where(id_lane == k, asked, id_mat)
    for mm in range(na):
        cm[mm, 0:NO, :] = pos_by[mm * NO:(mm + 1) * NO, :]
        cm[mm, NO:NO + 1, :] = id_mat[mm:mm + 1, :]

    bk = bk_ref[...]
    inv = jnp.zeros((IBD, BLK), F32)
    for b in range(16):
        inv = inv + jnp.where(bk == b, 1.0 / jnp.full((IBD, BLK), prop_ref[0, b], F32), 0.0)
    invp[k0, 0:IBD, :] = inv * (2.0 * c)
    cr[m] = cm[m]

    def code_copy(i):
        mm = peer(i)
        return rc(cm.at[mm], cr.at[m], c_s.at[mm], c_r.at[m], zdev(mm))

    def az_copy(i):
        mm = peer(i)
        part = ua.at[m, pl.ds(q0, QR)]
        return rc(part, part, az_s.at[mm], az_r.at[m], zdev(mm))

    def ix_copy(xx):
        part = items.at[k0, pl.ds(h0, HB)]
        return rc(part, part, ix_s.at[xx], ix_r.at[x], xdev(xx))

    def ix_in(xx):
        part = items.at[own + xx, pl.ds(h0, HB)]
        return rc(part, part, ix_s.at[xx], ix_r.at[xx], xdev(xx))

    def iz_copy(k):
        part = items.at[k, pl.ds(h0, HB)]
        return rc(part, part, iz_s, iz_r, mate)

    def jz_copy(k, xx):
        part = items.at[k, pl.ds(h0 + ZB, HB - ZB)]
        return rc(part, part, jz_s.at[xx], jz_r.at[xx], mate)

    def jx_copy(xx):
        part = items.at[far + x, pl.ds(h0, ZB)]
        return rc(part, part, jx_s.at[xx], jx_r.at[x], xdev(xx))

    def jx_in(xx):
        part = items.at[far + xx, pl.ds(h0, ZB)]
        return rc(part, part, jx_s.at[xx], jx_r.at[xx], xdev(xx))

    def core_items(k, start):
        part = items.at[k, pl.ds(start, HB)]
        return rc(part, part, f_s.at[k], f_r.at[k], sib)

    def p_copy(k, xx, ss, rs, slot):
        return rc(invp.at[k], invp.at[k], ss.at[xx], rs.at[slot], xdev(xx))

    def pz_copy(k):
        return rc(invp.at[k], invp.at[k], pz_s, pz_r, mate)

    own_users.wait()
    own_items.wait()
    pl.semaphore_wait(barrier, na - 1 + NX - 1 + NY - 1 + 2)

    def send_users(i, carry):
        az_copy(i).start()
        return carry

    def send_codes(i, carry):
        code_copy(i).start()
        return carry

    for d in (2, 1, 3):
        ix_copy(off(x, d, NX)).start()
    lax.fori_loop(0, na - 1, send_users, 0)
    iz_copy(k0).start()
    lax.fori_loop(0, na - 1, send_codes, 0)
    for d in (2, 1, 3):
        xx = off(x, d, NX)
        p_copy(k0, xx, p_s, p_r, x).start()
    pz_copy(k0).start()

    def forward_y(buf, mm, ss, rs):
        part = buf.at[mm, pl.ds(q0, QR)]
        for d in (2, 1, 3):
            rc(part, part, ss.at[mm], rs.at[mm], ydev(off(y, d, NY))).start()

    def three(buf, mm, ss, rs):
        part = buf.at[mm, pl.ds(0, QR * (NY - 1))]
        return rc(part, part, ss.at[mm], rs.at[mm], ydev(off(y, 1, NY)))

    def arrive_z(buf, mm, ss, rs):
        part = buf.at[mm, pl.ds(q0, QR)]
        rc(part, part, ss.at[mm], rs.at[mm], zdev(mm)).wait_recv()

    def forward_first(i, carry):
        mm = source(na - 2 - i)
        arrive_z(ua, mm, az_s, az_r)
        forward_y(ua, mm, ay_s, ay_r)
        return carry

    lax.fori_loop(0, 4, forward_first, 0)
    iz_copy(far + x).wait_recv()
    for d in (2, 1, 3):
        jx_copy(off(x, d, NX)).start()
    core_items(far + x, h0).start()
    lax.fori_loop(4, na - 1, forward_first, 0)
    pz_copy(far + x).wait_recv()
    for d in (2, 1, 3):
        xx = off(x, d, NX)
        p_copy(far + x, xx, pf_s, pf_r, x).start()
    for d in (1, 3, 2):
        xx = off(x, d, NX)
        ix_in(xx).wait_recv()
        jz_copy(own + xx, xx).start()
        core_items(own + xx, h0).start()
    for d in (1, 3, 2):
        xx = off(x, d, NX)
        p_copy(own + xx, xx, p_s, p_r, xx).wait_recv()
        p_copy(far + xx, xx, pf_s, pf_r, xx).wait_recv()

    def take_codes(i, carry):
        mm = source(i)
        rc(cm.at[mm], cr.at[mm], c_s.at[mm], c_r.at[mm], zdev(mm)).wait_recv()
        return carry

    lax.fori_loop(0, na - 1, take_codes, 0)
    for mm in range(na):
        idv[mm:mm + 1, :] = cr[mm, NO:NO + 1, :]
    to_smem = pltpu.make_async_copy(idv, ids, sm_sem)
    to_smem.start()
    for k in range(NO):
        cols = jnp.transpose(invp[k])
        for j in range(IBD):
            invcol[k, j] = jnp.broadcast_to(cols[:, j:j + 1], (BLK, BLK))
            invrow[k, j] = jnp.broadcast_to(invp[k, j:j + 1, :], (8, BLK))
    for d in (1, 3, 2):
        xx = off(x, d, NX)
        jx_in(xx).wait_recv()
        jz_copy(far + xx, xx).wait_recv()
        core_items(far + xx, h0).start()
    to_smem.wait()
    o0 = (1 - r) * HB
    core_items(far + x, o0).wait_recv()
    for d in (1, 3, 2):
        xx = off(x, d, NX)
        core_items(own + xx, o0).wait_recv()
        core_items(far + xx, o0).wait_recv()

    lane_f = lax.broadcasted_iota(jnp.int32, (BLK, BLK), 1).astype(F32)
    sub = lax.broadcasted_iota(jnp.int32, (BLK, BLK), 0)

    def pick(mm, k):
        code = ids[mm, k]
        j = jnp.maximum(code - 1, 0)
        flat = jnp.where(code > 0, 2.0 * c, 0.0).astype(F32)
        return code, j, items[k, j], flat

    def grads(mm):
        users = ua[mm]
        cols = jnp.transpose(cr[mm, 0:NO, :].astype(F32))
        total = jnp.zeros((BLK, RANK), F32)
        for part in range(NO // NX):
            picks = [pick(mm, part * NX + q) for q in range(NX)]
            stack = jnp.concatenate([t[2] for t in picks], axis=0)
            scores = nt(users, stack)
            hs = []
            for q in range(NX):
                k = part * NX + q
                code, j, block, flat = picks[q]
                s = scores[:, q * BLK:(q + 1) * BLK]
                hit = cols[:, k:k + 1] == lane_f
                w = invrow[k, j][0:1, :]
                margin = jnp.maximum(1.0 + s * jnp.where(hit, -c, c), 0.0)
                hs.append((margin * jnp.where(hit, -w, flat)).astype(BF16))
            total = total + nn(jnp.concatenate(hs, axis=1), stack)
        return total

    def ry_copy(mm, d):
        yy = off(y, d, NY)
        return rc(gs.at[mm, pl.ds(pl.multiple_of(yy * QR, QR), QR)], yr.at[mm, pl.ds(q0, QR)],
                  ry_s.at[mm], ry_r.at[mm], ydev(yy))

    def rz_copy(mm):
        return rc(zs_buf.at[mm], zr.at[m], rz_s.at[mm], rz_r.at[m], zdev(mm))

    def sum_y(mm):
        part = yr.at[mm, pl.ds(0, QR * (NY - 1))]
        rc(part, part, ry_s.at[mm], ry_r.at[mm], ydev(off(y, 1, NY))).wait_recv()
        total = gs[mm, pl.ds(q0, QR), :].astype(F32)
        for d in range(1, NY):
            total = total + yr[mm, pl.ds(pl.multiple_of(off(y, d, NY) * QR, QR), QR), :].astype(F32)
        return total

    def first_pass(i, carry):
        @pl.when(i < na)
        def _():
            mm = peer(i)

            @pl.when(i < na - 1)
            def _():
                three(ua, mm, ay_s, ay_r).wait_recv()

            gs[mm] = grads(mm).astype(BF16)
            for d in (2, 1, 3):
                ry_copy(mm, d).start()

        @pl.when(i >= LAG1)
        def _():
            mm = peer(i - LAG1)
            total = sum_y(mm)

            @pl.when(i < na - 1 + LAG1)
            def _():
                zs_buf[mm] = total.astype(BF16)
                rz_copy(mm).start()

            @pl.when(i == na - 1 + LAG1)
            def _():
                own_sum[...] = total

        return carry

    lax.fori_loop(0, na + LAG1, first_pass, 0)

    def gather_sum(i, carry):
        mm = source(i)
        rc(zs_buf.at[mm], zr.at[mm], rz_s.at[mm], rz_r.at[mm], zdev(mm)).wait_recv()
        own_sum[...] += zr[mm].astype(F32)
        return carry

    lax.fori_loop(0, na - 1, gather_sum, 0)

    old = ua[m, pl.ds(q0, QR), :].astype(F32)
    ub[m, pl.ds(q0, QR), :] = (old - STEP_USER * (own_sum[...] + DECAY * old)).astype(BF16)

    def bz_copy(i):
        mm = peer(i)
        part = ub.at[m, pl.ds(q0, QR)]
        return rc(part, part, bz_s.at[mm], bz_r.at[m], zdev(mm))

    def send_new(i, carry):
        bz_copy(i).start()
        return carry

    lax.fori_loop(0, na - 1, send_new, 0)
    forward_y(ub, m, by_s, by_r)

    def expand(mm):
        users = ub[mm]
        z0 = pl.multiple_of(mm * BLK, BLK)
        for k in range(NO):
            code, j, block, flat = pick(mm, k)
            s = nt(block, users)
            hit = cr[mm, k:k + 1, :] == sub
            margin = jnp.maximum(1.0 + s * jnp.where(hit, -c, c), 0.0)
            h = margin * jnp.where(hit, -invcol[k, j], flat)
            for jj in range(IBD):
                hexp[k, jj * BLK:(jj + 1) * BLK, pl.ds(z0, BLK)] = jnp.where(code == jj + 1, h, 0.0).astype(BF16)

    def second_pass(i, carry):
        @pl.when(jnp.logical_and(i > 0, i < na))
        def _():
            mm = source(na - 1 - i)
            arrive_z(ub, mm, bz_s, bz_r)
            forward_y(ub, mm, by_s, by_r)

        @pl.when(i >= LAG2)
        def _():
            mm = source(na - 1 - (i - LAG2))
            three(ub, mm, by_s, by_r).wait_recv()
            expand(mm)

        return carry

    lax.fori_loop(0, na + LAG2, second_pass, 0)

    ou_ref[pl.ds(b0, BLK), :] = ub[m]
    out_u = rc(ub.at[m], ou_ref.at[pl.ds(b0, BLK)], o_s.at[0], o_r.at[0], sib)
    out_u.start()

    flat_users = ub.reshape(na * BLK, RANK)

    def item_dot(k, h):
        rows = hexp[k, pl.ds(pl.multiple_of(h * HALF, HALF), HALF), :]
        return nn(rows, flat_users[...])

    def core_copy(k):
        return rc(cs.at[k], ccr.at[k], g_s.at[k], g_r.at[k], sib)

    def other_half(j, carry):
        k = lax.rem(far + NX * (j // NX), NO) + lax.rem(x + 1 + j, NX)
        cs[k] = item_dot(k, 1 - r).astype(BF16)
        core_copy(k).start()
        return carry

    lax.fori_loop(0, NO, other_half, 0)

    def w_copy(xx):
        return rc(xs.at[far + xx, pl.ds(0, ZROWS)], zrec.at[xx], w_s.at[xx], w_r.at[xx], mate)

    def w_in(xx):
        return rc(xs.at[own + xx, pl.ds(0, ZROWS)], zrec.at[xx], w_s.at[xx], w_r.at[xx], mate)

    def v_copy(xx):
        return rc(xs.at[far + xx, pl.ds(ZROWS, HALF - ZROWS)], xrec1.at[x], v_s.at[xx], v_r.at[x], xdev(xx))

    def x_copy(xx):
        return rc(xs.at[own + xx], xrec.at[x], x_s.at[xx], x_r.at[x], xdev(xx))

    def far_half(j, carry):
        xx = lax.rem(x + 1 + j, NX)
        k = far + xx
        mine = item_dot(k, r)
        core_copy(k).wait_recv()
        xs[k] = (mine + ccr[k].astype(F32)).astype(BF16)
        w_copy(xx).start()

        @pl.when(j < NX - 1)
        def _():
            v_copy(xx).start()

        return carry

    lax.fori_loop(0, NX, far_half, 0)

    def own_half(j, carry):
        xx = lax.rem(x + 1 + j, NX)
        k = own + xx
        mine = item_dot(k, r)
        core_copy(k).wait_recv()
        w_in(xx).wait_recv()
        total = mine + ccr[k].astype(F32)
        xs[k, pl.ds(0, ZROWS), :] = (total[0:ZROWS] + zrec[xx].astype(F32)).astype(BF16)
        xs[k, pl.ds(ZROWS, HALF - ZROWS), :] = total[ZROWS:].astype(BF16)

        @pl.when(j < NX - 1)
        def _():
            x_copy(xx).start()

        return carry

    lax.fori_loop(0, NX, own_half, 0)

    part = xs[far + x, pl.ds(ZROWS, HALF - ZROWS), :].astype(F32)
    for d in (1, 3, 2):
        xx = off(x, d, NX)
        rc(xrec1.at[xx], xrec1.at[xx], v_s.at[xx], v_r.at[xx], xdev(xx)).wait_recv()
        part = part + xrec1[xx].astype(F32)
    psum[...] = part.astype(BF16)
    to_mate = rc(psum, prec, t_s, t_r, mate)
    to_mate.start()

    for d in (1, 3, 2):
        xx = off(x, d, NX)
        rc(xrec.at[xx], xrec.at[xx], x_s.at[xx], x_r.at[xx], xdev(xx)).wait_recv()
    to_mate.wait_recv()
    for b in range(HB):
        rows = pl.ds(b * BLK, BLK)
        total = xs[k0, rows, :].astype(F32)
        for d in range(1, NX):
            total = total + xrec[off(x, d, NX), rows, :].astype(F32)
        if b >= ZB2:
            total = total + prec[pl.ds((b - ZB2) * BLK, BLK), :].astype(F32)
        olds = items[k0, h0 + b].astype(F32)
        oi_ref[h0 + b] = (olds - STEP_ITEM * (total + DECAY * olds)).astype(BF16)
    mine = oi_ref.at[pl.ds(h0, HB)]
    out_i = rc(mine, mine, o_s.at[1], o_r.at[1], sib)
    out_i.start()

    iz_copy(k0).wait_send()
    pz_copy(k0).wait_send()
    to_mate.wait_send()
    core_items(far + x, h0).wait_send()
    for d in range(NX):
        xx = off(x, d, NX)
        core_copy(own + xx).wait_send()
        core_copy(far + xx).wait_send()
        w_copy(xx).wait_send()
        if d:
            ix_copy(xx).wait_send()
            jx_copy(xx).wait_send()
            jz_copy(own + xx, xx).wait_send()
            core_items(own + xx, h0).wait_send()
            core_items(far + xx, h0).wait_send()
            p_copy(k0, xx, p_s, p_r, x).wait_send()
            p_copy(far + x, xx, pf_s, pf_r, x).wait_send()
            v_copy(xx).wait_send()
            x_copy(xx).wait_send()

    def sent(i, carry):
        code_copy(i).wait_send()
        az_copy(i).wait_send()
        bz_copy(i).wait_send()
        mm = peer(i)
        three(ua, mm, ay_s, ay_r).wait_send()
        rz_copy(mm).wait_send()
        return carry

    lax.fori_loop(0, na - 1, sent, 0)

    def sent_all(i, carry):
        three(ub, i, by_s, by_r).wait_send()
        three(gs, i, ry_s, ry_r).wait_send()
        return carry

    lax.fori_loop(0, na, sent_all, 0)
    out_u.wait_send()
    out_i.wait_send()
    other_b = pl.multiple_of((1 - r) * BLK, BLK)
    rc(ub.at[m], ou_ref.at[pl.ds(other_b, BLK)], o_s.at[0], o_r.at[0], sib).wait_recv()
    theirs = oi_ref.at[pl.ds(o0, HB)]
    rc(theirs, theirs, o_s.at[1], o_r.at[1], sib).wait_recv()


def body(na, user_factors, item_factors, item_bucket, propensity, tile_blocks, positives):
    dma = pltpu.SemaphoreType.DMA
    V = pltpu.VMEM
    scratch = [
        V((na, 16, BLK), jnp.int32),
        V((na, 16, BLK), jnp.int32),
        V((na, BLK), jnp.int32),
        pltpu.SMEM((na, BLK), jnp.int32),
        V((NO, IBD, BLK, RANK), BF16),
        V((NO, 8, BLK), F32),
        V((NO, IBD, 8, BLK), F32),
        V((NO, IBD, BLK, BLK), F32),
        V((na, BLK, RANK), BF16),
        V((na, BLK, RANK), BF16),
        V((na, BLK, RANK), BF16),
        V((na, BLK, RANK), BF16),
        V((na, QR, RANK), BF16),
        V((na, QR, RANK), BF16),
        V((NO, IBD * BLK, na * BLK), BF16),
        V((NO, HALF, RANK), BF16),
        V((NO, HALF, RANK), BF16),
        V((NO, HALF, RANK), BF16),
        V((NX, ZROWS, RANK), BF16),
        V((NX, HALF, RANK), BF16),
        V((NX, HALF - ZROWS, RANK), BF16),
        V((HALF - ZROWS, RANK), BF16),
        V((HALF - ZROWS, RANK), BF16),
        V((QR, RANK), F32),
        dma((na,)), dma((na,)), dma,
        dma((NX,)), dma((NX,)), dma, dma, dma((NX,)), dma((NX,)), dma((NX,)), dma((NX,)), dma((NO,)), dma((NO,)),
        dma((NX,)), dma((NX,)), dma, dma, dma((NX,)), dma((NX,)),
        dma((na,)), dma((na,)), dma((na,)), dma((na,)),
        dma((na,)), dma((na,)), dma((na,)), dma((na,)),
        dma((na,)), dma((na,)), dma((na,)), dma((na,)),
        dma((NO,)), dma((NO,)), dma((NX,)), dma((NX,)), dma((NX,)), dma((NX,)), dma((NX,)), dma((NX,)), dma, dma,
        dma((2,)), dma((2,)), dma((2,)),
    ]
    vmem = pl.BlockSpec(memory_space=pltpu.VMEM)
    anywhere = pl.BlockSpec(memory_space=pl.ANY)
    new_users, new_items = pl.pallas_call(
        functools.partial(kernel, na),
        out_shape=(
            jax.ShapeDtypeStruct(user_factors.shape, BF16),
            jax.ShapeDtypeStruct((IBD, BLK, RANK), BF16),
        ),
        in_specs=[anywhere, anywhere, vmem, pl.BlockSpec(memory_space=pltpu.SMEM), vmem, vmem],
        out_specs=(vmem, vmem),
        scratch_shapes=scratch,
        compiler_params=pltpu.CompilerParams(
            collective_id=0, has_side_effects=True, vmem_limit_bytes=56 << 20),
    )(
        user_factors,
        item_factors.reshape(IBD, BLK, RANK),
        item_bucket.reshape(IBD, BLK),
        propensity.reshape(1, -1),
        tile_blocks,
        positives.T,
    )
    return new_users, new_items.reshape(item_factors.shape)


def solution(mesh):
    na = mesh.shape["user"] // NX // 2
    return jax.shard_map(
        functools.partial(body, na),
        mesh=mesh,
        in_specs=(
            P("user", None),
            P(("user", "item"), None),
            P(("user", "item")),
            P(),
            P("user", "item"),
            P("user", "item"),
        ),
        out_specs=(P("user", None), P(("user", "item"), None)),
        check_vma=False,
    )
```

time: 594 us -> 102 us (0.17)
  waiting for transfers between devices: 284 us -> 0 us
  blocking collectives: 233 us -> 0 us
  Pallas kernels: 0 us -> 97.5 us
  local copies, waits for them, and re-layouts: 29.2 us -> 3.33 us
  other arithmetic: 18.8 us -> 0 us
  between operations: 14.2 us -> 0.64 us
  starting transfers between devices: 10.3 us -> 0 us
    all_to_all x2 -> x0, blocking collectives: 231 us -> none  [the longest x1 199 us: body(): lax.all_to_all(panels.astype(jnp.bfloat16), 'user', split_axis=0, concat_...]
    all_to_all x2 -> x0, waiting for transfers between devices: 192 us -> none  [the longest x1 183 us: body(): lax.all_to_all(item_stack[picked], 'user', split_axis=0, concat_axis=0, t...]
    pallas_call x0 -> x1, Pallas kernels: none -> 97.5 us  [body(): pl.pallas_call(functools.partial(kernel, na), out_shape=(jax.ShapeDtypeSt...]
    psum x1 -> x0, waiting for transfers between devices: 73 us -> none  [body(): grad_total = lax.psum(user_partial, ('item', 'rep'))]
    gather x10 -> x0, local copies, waits for them, and re-layouts: 19.1 us -> none  [the longest x4 11.2 us: tile_terms(): item_tiles = fetched[owners]]
    reduce_scatter x1 -> x0, waiting for transfers between devices: 18.2 us -> none  [body(): lax.psum_scatter(grad_local.astype(jnp.bfloat16), 'rep', scatter_dimensio...]
    all_to_all x2 -> x0, starting transfers between devices: 10.3 us -> none  [the longest x1 5.67 us: body(): lax.all_to_all(item_stack[picked], 'user', split_axis=0, concat_axis=0, t...]
    scatter-add x2 -> x0, other arithmetic: 9.23 us -> none  [second_pass(): return (panels.at[owners].add(item_terms), None)]
  transfers between devices with their start and end apart: 4 -> 0, of which waited for: 4 -> 0; matrix products, arithmetic and copies ran while one was open for 1% -> 0% of each run, Pallas kernels for 0% -> 0%
where the time goes in v2:
time: 102 us; the launch traced here: 101 us
  Pallas kernels  97.5 us (96%)
  local copies, waits for them, and re-layouts  3.33 us (3%)
    pallas_call x1, Pallas kernels, body(): pl.pallas_call(functools.partial(kernel, na), out_shape=(jax.ShapeDtypeSt...  97.5 us
    unnamed x2, local copies, waits for them, and re-layouts  3.33 us

profile of v2, /device:TPU:1, one launch (start us, length us, event | category | flops | bytes accessed | tf_op | source)
XLA Modules:
  0.0 101.5 jit_solution(6550360007662790937)
XLA Ops:
  0.6 97.5 %shard_map.77 = (bf16[256,256]{1,0:T(8,128)(2,1)}, bf16[6,128,256]{2,1,0:T(8,128)(2,1)}) custom-call(bf16[256,256]{1,0:T(8,128)(2,1)} %u_ref.1, bf16[6,128,256]{2,1,0:T(8,128)(2,1)} %bitcast.5, s32[6,128]{1,0:T(8,128)} %bitcast.8, f32[1,16]{1,0:T(1,128)} %bitcast.9, s32[2,32]{1,0:T(2,128)} %tb_ref.1, s32[32,256]{1,0:T(8,128)} %bitcast.7), custom_call_target="tpu_custom_call" | custom-call | tf_op jit(solution)/shard_map/pallas_call | solution.py:573
  98.2 1.6 %copy.10 = bf16[256,256]{1,0:T(8,128)(2,1)} copy(bf16[256,256]{1,0:T(8,128)(2,1)} %get-tuple-element.8) | data formatting | bytes 262144
  99.7 1.8 %copy.11 = bf16[768,256]{1,0:T(8,128)(2,1)} copy(bf16[768,256]{1,0:T(8,128)(2,1)} %bitcast.6) | data formatting | bytes 786432

commit v3 on v2

--- a/solution.py
+++ b/solution.py
@@ -24,10 +24,10 @@
 QR = BLK // NY
 NO = 2 * NX
 ZB = 2
-ZB2 = 2
+ZB2 = 1
 ZROWS = ZB2 * BLK
 LAG1 = 4
-LAG2 = 3
+LAG2 = 5
 
 
 def nt(a, b):
@@ -39,12 +39,12 @@
 
 
 def kernel(na, u_ref, it_ref, bk_ref, prop_ref, tb_ref, pos_ref, ou_ref, oi_ref,
-           cm, cr, idv, ids, items, invp, invrow, invcol, ua, ub, gs, yr, zs_buf, zr, hexp,
+           cm, cr, idv, ids, items, invp, invrow, invcol, ua, ub, gs, yr, zs_buf, zr, slot, prv, lst,
            cs, ccr, xs, zrec, xrec, xrec1, psum, prec, own_sum,
            c_s, c_r, sm_sem, ix_s, ix_r, iz_s, iz_r, jx_s, jx_r, jz_s, jz_r, f_s, f_r,
            p_s, p_r, pz_s, pz_r, pf_s, pf_r,
            az_s, az_r, ay_s, ay_r, ry_s, ry_r, rz_s, rz_r, bz_s, bz_r, by_s, by_r,
-           g_s, g_r, x_s, x_r, w_s, w_r, v_s, v_r, t_s, t_r, o_s, o_r, l_sem):
+           g_s, g_r, x_s, x_r, xb_s, xb_r, w_s, w_r, v_s, v_r, t_s, t_r, o_s, o_r, l_sem):
     user = lax.axis_index("user")
     y = lax.axis_index("item")
     r = lax.axis_index("rep")
@@ -188,10 +188,10 @@
         code_copy(i).start()
         return carry
 
-    for d in (2, 1, 3):
+    iz_copy(k0).start()
+    for d in (1, 3, 2):
         ix_copy(off(x, d, NX)).start()
     lax.fori_loop(0, na - 1, send_users, 0)
-    iz_copy(k0).start()
     lax.fori_loop(0, na - 1, send_codes, 0)
     for d in (2, 1, 3):
         xx = off(x, d, NX)
@@ -217,21 +217,25 @@
         forward_y(ua, mm, ay_s, ay_r)
         return carry
 
-    lax.fori_loop(0, 4, forward_first, 0)
+    def forward_own(xx):
+        ix_in(xx).wait_recv()
+        jz_copy(own + xx, xx).start()
+        core_items(own + xx, h0).start()
+
     iz_copy(far + x).wait_recv()
     for d in (2, 1, 3):
         jx_copy(off(x, d, NX)).start()
     core_items(far + x, h0).start()
-    lax.fori_loop(4, na - 1, forward_first, 0)
+    lax.fori_loop(0, 2, forward_first, 0)
+    forward_own(off(x, 1, NX))
+    forward_own(off(x, 3, NX))
+    lax.fori_loop(2, 4, forward_first, 0)
+    forward_own(off(x, 2, NX))
     pz_copy(far + x).wait_recv()
     for d in (2, 1, 3):
         xx = off(x, d, NX)
         p_copy(far + x, xx, pf_s, pf_r, x).start()
-    for d in (1, 3, 2):
-        xx = off(x, d, NX)
-        ix_in(xx).wait_recv()
-        jz_copy(own + xx, xx).start()
-        core_items(own + xx, h0).start()
+    lax.fori_loop(4, na - 1, forward_first, 0)
     for d in (1, 3, 2):
         xx = off(x, d, NX)
         p_copy(own + xx, xx, p_s, p_r, xx).wait_recv()
@@ -252,12 +256,29 @@
         for j in range(IBD):
             invcol[k, j] = jnp.broadcast_to(cols[:, j:j + 1], (BLK, BLK))
             invrow[k, j] = jnp.broadcast_to(invp[k, j:j + 1, :], (8, BLK))
+    to_smem.wait()
+
+    def chain(k, carry):
+        codes = [ids[source(na - 1 - i), k] for i in range(na)]
+        for i in range(na):
+            before = 0
+            for e in range(i):
+                before = jnp.where(codes[e] == codes[i], e + 1, before)
+            prv[k, i] = jnp.int32(before)
+        for j in range(IBD):
+            last = 0
+            for i in range(na):
+                last = jnp.where(codes[i] == j + 1, i + 1, last)
+            lst[k, j] = last
+        slot[k, 0] = jnp.zeros((BLK, RANK), F32)
+        return carry
+
+    lax.fori_loop(0, NO, chain, 0)
     for d in (1, 3, 2):
         xx = off(x, d, NX)
         jx_in(xx).wait_recv()
         jz_copy(far + xx, xx).wait_recv()
         core_items(far + xx, h0).start()
-    to_smem.wait()
     o0 = (1 - r) * HB
     core_items(far + x, o0).wait_recv()
     for d in (1, 3, 2):
@@ -364,17 +385,23 @@
     lax.fori_loop(0, na - 1, send_new, 0)
     forward_y(ub, m, by_s, by_r)
 
-    def expand(mm):
+    def expand(i, mm):
         users = ub[mm]
-        z0 = pl.multiple_of(mm * BLK, BLK)
-        for k in range(NO):
-            code, j, block, flat = pick(mm, k)
-            s = nt(block, users)
-            hit = cr[mm, k:k + 1, :] == sub
-            margin = jnp.maximum(1.0 + s * jnp.where(hit, -c, c), 0.0)
-            h = margin * jnp.where(hit, -invcol[k, j], flat)
-            for jj in range(IBD):
-                hexp[k, jj * BLK:(jj + 1) * BLK, pl.ds(z0, BLK)] = jnp.where(code == jj + 1, h, 0.0).astype(BF16)
+        for part in range(NO // NX):
+            picks = [pick(mm, part * NX + q) for q in range(NX)]
+            scores = nt(jnp.concatenate([t[2] for t in picks], axis=0), users)
+            hs = []
+            for q in range(NX):
+                k = part * NX + q
+                code, j, block, flat = picks[q]
+                s = scores[q * BLK:(q + 1) * BLK]
+                hit = cr[mm, k:k + 1, :] == sub
+                margin = jnp.maximum(1.0 + s * jnp.where(hit, -c, c), 0.0)
+                hs.append((margin * jnp.where(hit, -invcol[k, j], flat)).astype(BF16))
+            terms = nn(jnp.concatenate(hs, axis=0), users)
+            for q in range(NX):
+                k = part * NX + q
+                slot[k, i + 1] = terms[q * BLK:(q + 1) * BLK] + slot[k, prv[k, i]]
 
     def second_pass(i, carry):
         @pl.when(jnp.logical_and(i > 0, i < na))
@@ -387,7 +414,7 @@
         def _():
             mm = source(na - 1 - (i - LAG2))
             three(ub, mm, by_s, by_r).wait_recv()
-            expand(mm)
+            expand(i - LAG2, mm)
 
         return carry
 
@@ -397,22 +424,26 @@
     out_u = rc(ub.at[m], ou_ref.at[pl.ds(b0, BLK)], o_s.at[0], o_r.at[0], sib)
     out_u.start()
 
-    flat_users = ub.reshape(na * BLK, RANK)
-
-    def item_dot(k, h):
-        rows = hexp[k, pl.ds(pl.multiple_of(h * HALF, HALF), HALF), :]
-        return nn(rows, flat_users[...])
+    def item_sum(k, b):
+        return slot[k, lst[k, b]]
 
     def core_copy(k):
         return rc(cs.at[k], ccr.at[k], g_s.at[k], g_r.at[k], sib)
 
-    def other_half(j, carry):
-        k = lax.rem(far + NX * (j // NX), NO) + lax.rem(x + 1 + j, NX)
-        cs[k] = item_dot(k, 1 - r).astype(BF16)
+    def other_half(k):
+        for b in range(HB):
+            cs[k, b * BLK:(b + 1) * BLK, :] = item_sum(k, o0 + b).astype(BF16)
         core_copy(k).start()
-        return carry
-
-    lax.fori_loop(0, NO, other_half, 0)
+
+    def both(k):
+        core_copy(k).wait_recv()
+        for b in range(HB):
+            rows = slice(b * BLK, (b + 1) * BLK)
+            xs[k, rows, :] = (item_sum(k, h0 + b) + ccr[k, rows, :].astype(F32)).astype(BF16)
+
+    order = [off(x, d, NX) for d in (2, 1, 3, 0)]
+    for xx in order:
+        other_half(far + xx)
 
     def w_copy(xx):
         return rc(xs.at[far + xx, pl.ds(0, ZROWS)], zrec.at[xx], w_s.at[xx], w_r.at[xx], mate)
@@ -423,42 +454,33 @@
     def v_copy(xx):
         return rc(xs.at[far + xx, pl.ds(ZROWS, HALF - ZROWS)], xrec1.at[x], v_s.at[xx], v_r.at[x], xdev(xx))
 
-    def x_copy(xx):
-        return rc(xs.at[own + xx], xrec.at[x], x_s.at[xx], x_r.at[x], xdev(xx))
-
-    def far_half(j, carry):
-        xx = lax.rem(x + 1 + j, NX)
-        k = far + xx
-        mine = item_dot(k, r)
-        core_copy(k).wait_recv()
-        xs[k] = (mine + ccr[k].astype(F32)).astype(BF16)
+    def xa_copy(xx):
+        rows = pl.ds(ZROWS, HALF - ZROWS)
+        return rc(xs.at[own + xx, rows], xrec.at[x, rows], x_s.at[xx], x_r.at[x], xdev(xx))
+
+    def xb_copy(xx):
+        rows = pl.ds(0, ZROWS)
+        return rc(xs.at[own + xx, rows], xrec.at[x, rows], xb_s.at[xx], xb_r.at[x], xdev(xx))
+
+    for n, xx in enumerate(order):
+        other_half(own + xx)
+        both(far + xx)
         w_copy(xx).start()
-
-        @pl.when(j < NX - 1)
-        def _():
+        if n < NX - 1:
             v_copy(xx).start()
 
-        return carry
-
-    lax.fori_loop(0, NX, far_half, 0)
-
-    def own_half(j, carry):
-        xx = lax.rem(x + 1 + j, NX)
+    for n, xx in enumerate(order):
+        both(own + xx)
+        if n < NX - 1:
+            xa_copy(xx).start()
+
+    for n, xx in enumerate(order):
         k = own + xx
-        mine = item_dot(k, r)
-        core_copy(k).wait_recv()
         w_in(xx).wait_recv()
-        total = mine + ccr[k].astype(F32)
-        xs[k, pl.ds(0, ZROWS), :] = (total[0:ZROWS] + zrec[xx].astype(F32)).astype(BF16)
-        xs[k, pl.ds(ZROWS, HALF - ZROWS), :] = total[ZROWS:].astype(BF16)
-
-        @pl.when(j < NX - 1)
-        def _():
-            x_copy(xx).start()
-
-        return carry
-
-    lax.fori_loop(0, NX, own_half, 0)
+        rows = pl.ds(0, ZROWS)
+        xs[k, rows, :] = (xs[k, rows, :].astype(F32) + zrec[xx].astype(F32)).astype(BF16)
+        if n < NX - 1:
+            xb_copy(xx).start()
 
     part = xs[far + x, pl.ds(ZROWS, HALF - ZROWS), :].astype(F32)
     for d in (1, 3, 2):
@@ -471,7 +493,9 @@
 
     for d in (1, 3, 2):
         xx = off(x, d, NX)
-        rc(xrec.at[xx], xrec.at[xx], x_s.at[xx], x_r.at[xx], xdev(xx)).wait_recv()
+        lower, upper = xrec.at[xx, pl.ds(0, ZROWS)], xrec.at[xx, pl.ds(ZROWS, HALF - ZROWS)]
+        rc(upper, upper, x_s.at[xx], x_r.at[xx], xdev(xx)).wait_recv()
+        rc(lower, lower, xb_s.at[xx], xb_r.at[xx], xdev(xx)).wait_recv()
     to_mate.wait_recv()
     for b in range(HB):
         rows = pl.ds(b * BLK, BLK)
@@ -504,7 +528,8 @@
             p_copy(k0, xx, p_s, p_r, x).wait_send()
             p_copy(far + x, xx, pf_s, pf_r, x).wait_send()
             v_copy(xx).wait_send()
-            x_copy(xx).wait_send()
+            xa_copy(xx).wait_send()
+            xb_copy(xx).wait_send()
 
     def sent(i, carry):
         code_copy(i).wait_send()
@@ -549,7 +574,9 @@
         V((na, BLK, RANK), BF16),
         V((na, QR, RANK), BF16),
         V((na, QR, RANK), BF16),
-        V((NO, IBD * BLK, na * BLK), BF16),
+        V((NO, na + 1, BLK, RANK), F32),
+        pltpu.SMEM((NO, na), jnp.int32),
+        pltpu.SMEM((NO, IBD), jnp.int32),
         V((NO, HALF, RANK), BF16),
         V((NO, HALF, RANK), BF16),
         V((NO, HALF, RANK), BF16),
@@ -565,7 +592,8 @@
         dma((na,)), dma((na,)), dma((na,)), dma((na,)),
         dma((na,)), dma((na,)), dma((na,)), dma((na,)),
         dma((na,)), dma((na,)), dma((na,)), dma((na,)),
-        dma((NO,)), dma((NO,)), dma((NX,)), dma((NX,)), dma((NX,)), dma((NX,)), dma((NX,)), dma((NX,)), dma, dma,
+        dma((NO,)), dma((NO,)), dma((NX,)), dma((NX,)), dma((NX,)), dma((NX,)),
+        dma((NX,)), dma((NX,)), dma((NX,)), dma((NX,)), dma, dma,
         dma((2,)), dma((2,)), dma((2,)),
     ]
     vmem = pl.BlockSpec(memory_space=pltpu.VMEM)

time: 102 us -> 94.9 us (0.930)
  Pallas kernels: 97.5 us -> 90.7 us
    pallas_call x1, Pallas kernels: 97.5 us -> 90.7 us  [body(): pl.pallas_call(functools.partial(kernel, na), out_shape=(jax.ShapeDtypeSt...]
where the time goes in v3:
time: 94.9 us; the launch traced here: 94.6 us
  Pallas kernels  90.7 us (96%)
  local copies, waits for them, and re-layouts  3.33 us (4%)
    pallas_call x1, Pallas kernels, body(): pl.pallas_call(functools.partial(kernel, na), out_shape=(jax.ShapeDtypeSt...  90.7 us
    unnamed x2, local copies, waits for them, and re-layouts  3.33 us

profile of v3, /device:TPU:1, one launch (start us, length us, event | category | flops | bytes accessed | tf_op | source)
XLA Modules:
  0.0 94.6 jit_solution(2133851823678592793)
XLA Ops:
  0.6 90.7 %shard_map.77 = (bf16[256,256]{1,0:T(8,128)(2,1)}, bf16[6,128,256]{2,1,0:T(8,128)(2,1)}) custom-call(bf16[256,256]{1,0:T(8,128)(2,1)} %u_ref.1, bf16[6,128,256]{2,1,0:T(8,128)(2,1)} %bitcast.5, s32[6,128]{1,0:T(8,128)} %bitcast.8, f32[1,16]{1,0:T(1,128)} %bitcast.9, s32[2,32]{1,0:T(2,128)} %tb_ref.1, s32[32,256]{1,0:T(8,128)} %bitcast.7), custom_call_target="tpu_custom_call" | custom-call | tf_op jit(solution)/shard_map/pallas_call | solution.py:601
  91.3 1.6 %copy.10 = bf16[256,256]{1,0:T(8,128)(2,1)} copy(bf16[256,256]{1,0:T(8,128)(2,1)} %get-tuple-element.8) | data formatting | bytes 262144
  92.9 1.8 %copy.11 = bf16[768,256]{1,0:T(8,128)(2,1)} copy(bf16[768,256]{1,0:T(8,128)(2,1)} %bitcast.6) | data formatting | bytes 786432

commit v4 on v3

--- a/solution.py
+++ b/solution.py
@@ -24,8 +24,8 @@
 QR = BLK // NY
 NO = 2 * NX
 ZB = 2
-ZB2 = 1
-ZROWS = ZB2 * BLK
+ZROWS = 3 * BLK // 2
+CUT = BLK // 2
 LAG1 = 4
 LAG2 = 5
 
@@ -38,10 +38,11 @@
     return lax.dot_general(a, b, (((1,), (0,)), ((), ())), preferred_element_type=F32)
 
 
-def kernel(na, u_ref, it_ref, bk_ref, prop_ref, tb_ref, pos_ref, ou_ref, oi_ref,
+def kernel(na, u_ref, it_ref, bk_in, prop_in, tb_in, pos_in, ou_ref, oi_ref,
+           bk_ref, prop_ref, tb_ref, pos_ref,
            cm, cr, idv, ids, items, invp, invrow, invcol, ua, ub, gs, yr, zs_buf, zr, slot, prv, lst,
-           cs, ccr, xs, zrec, xrec, xrec1, psum, prec, own_sum,
-           c_s, c_r, sm_sem, ix_s, ix_r, iz_s, iz_r, jx_s, jx_r, jz_s, jz_r, f_s, f_r,
+           cs, ccr, xs, zrec, xrec, xrec1, psum, prec, own_sum, fin,
+           c_s, c_r, sm_sem, ix_s, ix_r, iz_s, iz_r, jx_s, jx_r, jz_s, jz_r, f_s, f_r, e_s, e_r,
            p_s, p_r, pz_s, pz_r, pf_s, pf_r,
            az_s, az_r, ay_s, ay_r, ry_s, ry_r, rz_s, rz_r, bz_s, bz_r, by_s, by_r,
            g_s, g_r, x_s, x_r, xb_s, xb_r, w_s, w_r, v_s, v_r, t_s, t_r, o_s, o_r, l_sem):
@@ -106,6 +107,13 @@
     own_items.start()
     own_users = pltpu.make_async_copy(u_ref.at[pl.ds(b0, BLK)], ua.at[m], l_sem.at[1])
     own_users.start()
+
+    small = [pltpu.make_async_copy(a, b, l_sem.at[2 + n]) for n, (a, b) in enumerate(
+        ((tb_in, tb_ref), (pos_in, pos_ref), (bk_in, bk_ref), (prop_in, prop_ref)))]
+    for copy in small:
+        copy.start()
+    for copy in small:
+        copy.wait()
 
     tb = tb_ref[pl.ds(r, 1), :]
     owner = (tb * 2731) >> 16
@@ -170,6 +178,15 @@
         part = items.at[k, pl.ds(start, HB)]
         return rc(part, part, f_s.at[k], f_r.at[k], sib)
 
+    def core_part(k, start, count, ss, rs):
+        part = items.at[k, pl.ds(start, count)]
+        return rc(part, part, ss, rs, sib)
+
+    def core_far(xx, start, last):
+        if last:
+            return core_part(far + xx, start + ZB, HB - ZB, e_s.at[xx], e_r.at[xx])
+        return core_part(far + xx, start, ZB, f_s.at[far + xx], f_r.at[far + xx])
+
     def p_copy(k, xx, ss, rs, slot):
         return rc(invp.at[k], invp.at[k], ss.at[xx], rs.at[slot], xdev(xx))
 
@@ -252,39 +269,25 @@
     to_smem = pltpu.make_async_copy(idv, ids, sm_sem)
     to_smem.start()
     for k in range(NO):
-        cols = jnp.transpose(invp[k])
         for j in range(IBD):
-            invcol[k, j] = jnp.broadcast_to(cols[:, j:j + 1], (BLK, BLK))
             invrow[k, j] = jnp.broadcast_to(invp[k, j:j + 1, :], (8, BLK))
     to_smem.wait()
 
-    def chain(k, carry):
-        codes = [ids[source(na - 1 - i), k] for i in range(na)]
-        for i in range(na):
-            before = 0
-            for e in range(i):
-                before = jnp.where(codes[e] == codes[i], e + 1, before)
-            prv[k, i] = jnp.int32(before)
-        for j in range(IBD):
-            last = 0
-            for i in range(na):
-                last = jnp.where(codes[i] == j + 1, i + 1, last)
-            lst[k, j] = last
-        slot[k, 0] = jnp.zeros((BLK, RANK), F32)
-        return carry
-
-    lax.fori_loop(0, NO, chain, 0)
     for d in (1, 3, 2):
         xx = off(x, d, NX)
+        jz_copy(far + xx, xx).wait_recv()
+        core_far(xx, h0, True).start()
+    for d in (1, 3, 2):
+        xx = off(x, d, NX)
         jx_in(xx).wait_recv()
-        jz_copy(far + xx, xx).wait_recv()
-        core_items(far + xx, h0).start()
+        core_far(xx, h0, False).start()
     o0 = (1 - r) * HB
     core_items(far + x, o0).wait_recv()
     for d in (1, 3, 2):
         xx = off(x, d, NX)
         core_items(own + xx, o0).wait_recv()
-        core_items(far + xx, o0).wait_recv()
+        core_far(xx, o0, True).wait_recv()
+        core_far(xx, o0, False).wait_recv()
 
     lane_f = lax.broadcasted_iota(jnp.int32, (BLK, BLK), 1).astype(F32)
     sub = lax.broadcasted_iota(jnp.int32, (BLK, BLK), 0)
@@ -362,6 +365,26 @@
 
     lax.fori_loop(0, na + LAG1, first_pass, 0)
 
+    def chain(k, carry):
+        codes = [ids[source(na - 1 - i), k] for i in range(na)]
+        for i in range(na):
+            before = 0
+            for e in range(i):
+                before = jnp.where(codes[e] == codes[i], e + 1, before)
+            prv[k, i] = jnp.int32(before)
+        for j in range(IBD):
+            last = 0
+            for i in range(na):
+                last = jnp.where(codes[i] == j + 1, i + 1, last)
+            lst[k, j] = last
+        cols = jnp.transpose(invp[k])
+        for j in range(IBD):
+            invcol[k, j] = jnp.broadcast_to(cols[:, j:j + 1], (BLK, BLK))
+        slot[k, 0] = jnp.zeros((BLK, RANK), F32)
+        return carry
+
+    lax.fori_loop(0, NO, chain, 0)
+
     def gather_sum(i, carry):
         mm = source(i)
         rc(zs_buf.at[mm], zr.at[mm], rz_s.at[mm], rz_r.at[mm], zdev(mm)).wait_recv()
@@ -379,7 +402,7 @@
         return rc(part, part, bz_s.at[mm], bz_r.at[m], zdev(mm))
 
     def send_new(i, carry):
-        bz_copy(i).start()
+        bz_copy(na - 2 - i).start()
         return carry
 
     lax.fori_loop(0, na - 1, send_new, 0)
@@ -420,7 +443,8 @@
 
     lax.fori_loop(0, na + LAG2, second_pass, 0)
 
-    ou_ref[pl.ds(b0, BLK), :] = ub[m]
+    keep_u = pltpu.make_async_copy(ub.at[m], ou_ref.at[pl.ds(b0, BLK)], l_sem.at[0])
+    keep_u.start()
     out_u = rc(ub.at[m], ou_ref.at[pl.ds(b0, BLK)], o_s.at[0], o_r.at[0], sib)
     out_u.start()
 
@@ -441,10 +465,6 @@
             rows = slice(b * BLK, (b + 1) * BLK)
             xs[k, rows, :] = (item_sum(k, h0 + b) + ccr[k, rows, :].astype(F32)).astype(BF16)
 
-    order = [off(x, d, NX) for d in (2, 1, 3, 0)]
-    for xx in order:
-        other_half(far + xx)
-
     def w_copy(xx):
         return rc(xs.at[far + xx, pl.ds(0, ZROWS)], zrec.at[xx], w_s.at[xx], w_r.at[xx], mate)
 
@@ -462,16 +482,20 @@
         rows = pl.ds(0, ZROWS)
         return rc(xs.at[own + xx, rows], xrec.at[x, rows], xb_s.at[xx], xb_r.at[x], xdev(xx))
 
-    for n, xx in enumerate(order):
-        other_half(own + xx)
-        both(far + xx)
-        w_copy(xx).start()
-        if n < NX - 1:
-            v_copy(xx).start()
-
-    for n, xx in enumerate(order):
-        both(own + xx)
-        if n < NX - 1:
+    order = [off(x, d, NX) for d in (2, 1, 3, 0)]
+    owners = [far + xx for xx in order] + [own + xx for xx in order]
+    other_half(owners[0])
+    other_half(owners[1])
+    for n, k in enumerate(owners):
+        if n + 2 < NO:
+            other_half(owners[n + 2])
+        both(k)
+        xx = order[n % NX]
+        if n < NX:
+            w_copy(xx).start()
+            if n < NX - 1:
+                v_copy(xx).start()
+        elif n < NO - 1:
             xa_copy(xx).start()
 
     for n, xx in enumerate(order):
@@ -497,18 +521,25 @@
         rc(upper, upper, x_s.at[xx], x_r.at[xx], xdev(xx)).wait_recv()
         rc(lower, lower, xb_s.at[xx], xb_r.at[xx], xdev(xx)).wait_recv()
     to_mate.wait_recv()
-    for b in range(HB):
-        rows = pl.ds(b * BLK, BLK)
+    def out_item(b, start):
+        return rc(fin.at[b], oi_ref.at[start + b], o_s.at[1 + b], o_r.at[1 + b], sib)
+
+    def keep_item(b):
+        return pltpu.make_async_copy(fin.at[b], oi_ref.at[h0 + b], l_sem.at[1 + b])
+
+    for b in range(2 * HB):
+        rows = pl.ds(b * CUT, CUT)
         total = xs[k0, rows, :].astype(F32)
         for d in range(1, NX):
             total = total + xrec[off(x, d, NX), rows, :].astype(F32)
-        if b >= ZB2:
-            total = total + prec[pl.ds((b - ZB2) * BLK, BLK), :].astype(F32)
-        olds = items[k0, h0 + b].astype(F32)
-        oi_ref[h0 + b] = (olds - STEP_ITEM * (total + DECAY * olds)).astype(BF16)
-    mine = oi_ref.at[pl.ds(h0, HB)]
-    out_i = rc(mine, mine, o_s.at[1], o_r.at[1], sib)
-    out_i.start()
+        if b * CUT >= ZROWS:
+            total = total + prec[pl.ds(b * CUT - ZROWS, CUT), :].astype(F32)
+        piece = pl.ds(b % 2 * CUT, CUT)
+        olds = items[k0, h0 + b // 2, piece, :].astype(F32)
+        fin[b // 2, piece, :] = (olds - STEP_ITEM * (total + DECAY * olds)).astype(BF16)
+        if b % 2:
+            out_item(b // 2, h0).start()
+            keep_item(b // 2).start()
 
     iz_copy(k0).wait_send()
     pz_copy(k0).wait_send()
@@ -524,7 +555,8 @@
             jx_copy(xx).wait_send()
             jz_copy(own + xx, xx).wait_send()
             core_items(own + xx, h0).wait_send()
-            core_items(far + xx, h0).wait_send()
+            core_far(xx, h0, True).wait_send()
+            core_far(xx, h0, False).wait_send()
             p_copy(k0, xx, p_s, p_r, x).wait_send()
             p_copy(far + x, xx, pf_s, pf_r, x).wait_send()
             v_copy(xx).wait_send()
@@ -549,17 +581,28 @@
 
     lax.fori_loop(0, na, sent_all, 0)
     out_u.wait_send()
-    out_i.wait_send()
+    keep_u.wait()
     other_b = pl.multiple_of((1 - r) * BLK, BLK)
     rc(ub.at[m], ou_ref.at[pl.ds(other_b, BLK)], o_s.at[0], o_r.at[0], sib).wait_recv()
-    theirs = oi_ref.at[pl.ds(o0, HB)]
-    rc(theirs, theirs, o_s.at[1], o_r.at[1], sib).wait_recv()
+    for b in range(HB):
+        keep_item(b).wait()
+        out_item(b, h0).wait_send()
+        out_item(b, o0).wait_recv()
+
+
+def hand_over(u_ref, i_ref, ou_ref, oi_ref):
+    ou_ref[...] = u_ref[...]
+    oi_ref[...] = i_ref[...]
 
 
 def body(na, user_factors, item_factors, item_bucket, propensity, tile_blocks, positives):
     dma = pltpu.SemaphoreType.DMA
     V = pltpu.VMEM
     scratch = [
+        V((IBD, BLK), jnp.int32),
+        pltpu.SMEM((1, propensity.shape[0]), F32),
+        V(tile_blocks.shape, jnp.int32),
+        V((positives.shape[1], positives.shape[0]), jnp.int32),
         V((na, 16, BLK), jnp.int32),
         V((na, 16, BLK), jnp.int32),
         V((na, BLK), jnp.int32),
@@ -586,15 +629,17 @@
         V((HALF - ZROWS, RANK), BF16),
         V((HALF - ZROWS, RANK), BF16),
         V((QR, RANK), F32),
+        V((HB, BLK, RANK), BF16),
         dma((na,)), dma((na,)), dma,
         dma((NX,)), dma((NX,)), dma, dma, dma((NX,)), dma((NX,)), dma((NX,)), dma((NX,)), dma((NO,)), dma((NO,)),
+        dma((NX,)), dma((NX,)),
         dma((NX,)), dma((NX,)), dma, dma, dma((NX,)), dma((NX,)),
         dma((na,)), dma((na,)), dma((na,)), dma((na,)),
         dma((na,)), dma((na,)), dma((na,)), dma((na,)),
         dma((na,)), dma((na,)), dma((na,)), dma((na,)),
         dma((NO,)), dma((NO,)), dma((NX,)), dma((NX,)), dma((NX,)), dma((NX,)),
         dma((NX,)), dma((NX,)), dma((NX,)), dma((NX,)), dma, dma,
-        dma((2,)), dma((2,)), dma((2,)),
+        dma((1 + HB,)), dma((1 + HB,)), dma((6,)),
     ]
     vmem = pl.BlockSpec(memory_space=pltpu.VMEM)
     anywhere = pl.BlockSpec(memory_space=pl.ANY)
@@ -604,8 +649,8 @@
             jax.ShapeDtypeStruct(user_factors.shape, BF16),
             jax.ShapeDtypeStruct((IBD, BLK, RANK), BF16),
         ),
-        in_specs=[anywhere, anywhere, vmem, pl.BlockSpec(memory_space=pltpu.SMEM), vmem, vmem],
-        out_specs=(vmem, vmem),
+        in_specs=[anywhere] * 6,
+        out_specs=(anywhere, anywhere),
         scratch_shapes=scratch,
         compiler_params=pltpu.CompilerParams(
             collective_id=0, has_side_effects=True, vmem_limit_bytes=56 << 20),
@@ -617,6 +662,15 @@
         tile_blocks,
         positives.T,
     )
+    new_users, new_items = pl.pallas_call(
+        hand_over,
+        out_shape=(
+            jax.ShapeDtypeStruct(user_factors.shape, BF16),
+            jax.ShapeDtypeStruct((IBD, BLK, RANK), BF16),
+        ),
+        in_specs=[vmem, vmem],
+        out_specs=(vmem, vmem),
+    )(new_users, new_items)
     return new_users, new_items.reshape(item_factors.shape)
 
 

time: 94.9 us -> 88.9 us (0.937)
  local copies, waits for them, and re-layouts: 3.33 us -> 0 us
  Pallas kernels: 90.7 us -> 88.1 us
    pallas_call x1, Pallas kernels: 90.7 us -> 86.3 us  [body(): pl.pallas_call(functools.partial(kernel, na), out_shape=(jax.ShapeDtypeSt...]
    unnamed x2 -> x0, local copies, waits for them, and re-layouts: 3.33 us -> none
    pallas_call x0 -> x1, Pallas kernels: none -> 1.87 us  [body(): pl.pallas_call(hand_over, out_shape=(jax.ShapeDtypeStruct(user_factors.sh...]
where the time goes in v4:
time: 88.9 us; the launch traced here: 88.8 us
  Pallas kernels  88.1 us (99%)
    pallas_call x1, Pallas kernels, body(): pl.pallas_call(functools.partial(kernel, na), out_shape=(jax.ShapeDtypeSt...  86.3 us
    pallas_call x1, Pallas kernels, body(): pl.pallas_call(hand_over, out_shape=(jax.ShapeDtypeStruct(user_factors.sh...  1.87 us

profile of v4, /device:TPU:1, one launch (start us, length us, event | category | flops | bytes accessed | tf_op | source)
XLA Modules:
  0.0 88.8 jit_solution(13734898824467046248)
XLA Ops:
  0.6 86.3 %shard_map.77 = (bf16[256,256]{1,0:T(8,128)(2,1)}, bf16[6,128,256]{2,1,0:T(8,128)(2,1)}) custom-call(bf16[256,256]{1,0:T(8,128)(2,1)} %u_ref.1, bf16[6,128,256]{2,1,0:T(8,128)(2,1)} %bitcast.5, s32[6,128]{1,0:T(8,128)} %bitcast.7, f32[1,16]{1,0:T(1,128)} %bitcast.8, s32[2,32]{1,0:T(2,128)} %tb_in.1, s32[32,256]{1,0:T(8,128)} %bitcast.6), custom_call_target="tpu_custom_call" | custom-call | tf_op jit(solution)/shard_map/pallas_call | solution.py:646
  86.9 1.9 %shard_map.78 = (bf16[256,256]{1,0:T(8,128)(2,1)}, bf16[6,128,256]{2,1,0:T(8,128)(2,1)}) custom-call(bf16[256,256]{1,0:T(8,128)(2,1)} %get-tuple-element.6.u_ref, bf16[6,128,256]{2,1,0:T(8,128)(2,1)} %get-tuple-element.7.i_ref), custom_call_target="tpu_custom_call" | custom-call | tf_op jit(solution)/shard_map/pallas_call | solution.py:665

commit v5 on v4

--- a/solution.py
+++ b/solution.py
@@ -119,20 +119,13 @@
     owner = (tb * 2731) >> 16
     local = tb - owner * (NY * IBD) - y * IBD
     ow_rows = lax.broadcasted_iota(jnp.int32, (na * NO, tb.shape[1]), 0)
-    hot = jnp.where(ow_rows == owner, 1.0, 0.0)
-    pos = pos_ref[:, pl.ds(b0, BLK)].astype(F32).astype(BF16)
-    pos_by = nn(hot.astype(BF16), pos)
-    named = jnp.sum(hot, axis=1, keepdims=True)
-    pos_by = jnp.where(named > 0.0, pos_by, -1.0).astype(jnp.int32)
-    m_rows = lax.broadcasted_iota(jnp.int32, (na, tb.shape[1]), 0)
-    id_lane = lax.broadcasted_iota(jnp.int32, (na, BLK), 1)
-    id_mat = jnp.zeros((na, BLK), jnp.int32)
-    for k in range(NO):
-        asked = jnp.max(jnp.where(owner == m_rows * NO + k, local + 1, 0), axis=1, keepdims=True)
-        id_mat = jnp.where(id_lane == k, asked, id_mat)
+    hot = jnp.where(ow_rows == owner, local + 1, 0)
+    packed = 256 * jnp.broadcast_to(jnp.max(hot, axis=1, keepdims=True), (na * NO, BLK))
+    for t in range(tb.shape[1]):
+        found = jnp.maximum(pos_ref[t:t + 1, pl.ds(b0, BLK)], -1) + 1
+        packed = packed + jnp.where(hot[:, t:t + 1] > 0, found, 0)
     for mm in range(na):
-        cm[mm, 0:NO, :] = pos_by[mm * NO:(mm + 1) * NO, :]
-        cm[mm, NO:NO + 1, :] = id_mat[mm:mm + 1, :]
+        cm[mm] = packed[mm * NO:(mm + 1) * NO, :]
 
     bk = bk_ref[...]
     inv = jnp.zeros((IBD, BLK), F32)
@@ -264,8 +257,9 @@
         return carry
 
     lax.fori_loop(0, na - 1, take_codes, 0)
+    idv[...] = jnp.zeros_like(idv)
     for mm in range(na):
-        idv[mm:mm + 1, :] = cr[mm, NO:NO + 1, :]
+        idv[mm:mm + 1, 0:NO] = jnp.transpose(cr[mm])[0:1, :]
     to_smem = pltpu.make_async_copy(idv, ids, sm_sem)
     to_smem.start()
     for k in range(NO):
@@ -293,14 +287,14 @@
     sub = lax.broadcasted_iota(jnp.int32, (BLK, BLK), 0)
 
     def pick(mm, k):
-        code = ids[mm, k]
+        code = ids[mm, k] >> 8
         j = jnp.maximum(code - 1, 0)
         flat = jnp.where(code > 0, 2.0 * c, 0.0).astype(F32)
         return code, j, items[k, j], flat
 
     def grads(mm):
         users = ua[mm]
-        cols = jnp.transpose(cr[mm, 0:NO, :].astype(F32))
+        cols = jnp.transpose(((cr[mm] & 255) - 1).astype(F32))
         total = jnp.zeros((BLK, RANK), F32)
         for part in range(NO // NX):
             picks = [pick(mm, part * NX + q) for q in range(NX)]
@@ -366,7 +360,7 @@
     lax.fori_loop(0, na + LAG1, first_pass, 0)
 
     def chain(k, carry):
-        codes = [ids[source(na - 1 - i), k] for i in range(na)]
+        codes = [ids[source(na - 1 - i), k] >> 8 for i in range(na)]
         for i in range(na):
             before = 0
             for e in range(i):
@@ -418,7 +412,7 @@
                 k = part * NX + q
                 code, j, block, flat = picks[q]
                 s = scores[q * BLK:(q + 1) * BLK]
-                hit = cr[mm, k:k + 1, :] == sub
+                hit = (cr[mm, k:k + 1, :] & 255) - 1 == sub
                 margin = jnp.maximum(1.0 + s * jnp.where(hit, -c, c), 0.0)
                 hs.append((margin * jnp.where(hit, -invcol[k, j], flat)).astype(BF16))
             terms = nn(jnp.concatenate(hs, axis=0), users)
@@ -603,8 +597,8 @@
         pltpu.SMEM((1, propensity.shape[0]), F32),
         V(tile_blocks.shape, jnp.int32),
         V((positives.shape[1], positives.shape[0]), jnp.int32),
-        V((na, 16, BLK), jnp.int32),
-        V((na, 16, BLK), jnp.int32),
+        V((na, NO, BLK), jnp.int32),
+        V((na, NO, BLK), jnp.int32),
         V((na, BLK), jnp.int32),
         pltpu.SMEM((na, BLK), jnp.int32),
         V((NO, IBD, BLK, RANK), BF16),

time: 88.9 us -> 87.9 us (0.989)
  Pallas kernels: 88.1 us -> 87.1 us
    pallas_call x1, Pallas kernels: 86.3 us -> 85.2 us  [body(): pl.pallas_call(functools.partial(kernel, na), out_shape=(jax.ShapeDtypeSt...]
where the time goes in v5:
time: 87.9 us; the launch traced here: 87.7 us
  Pallas kernels  87.1 us (99%)
    pallas_call x1, Pallas kernels, body(): pl.pallas_call(functools.partial(kernel, na), out_shape=(jax.ShapeDtypeSt...  85.2 us
    pallas_call x1, Pallas kernels, body(): pl.pallas_call(hand_over, out_shape=(jax.ShapeDtypeStruct(user_factors.sh...  1.87 us

profile of v5, /device:TPU:1, one launch (start us, length us, event | category | flops | bytes accessed | tf_op | source)
XLA Modules:
  0.0 87.7 jit_solution(15304952081908510698)
XLA Ops:
  0.6 85.2 %shard_map.77 = (bf16[256,256]{1,0:T(8,128)(2,1)}, bf16[6,128,256]{2,1,0:T(8,128)(2,1)}) custom-call(bf16[256,256]{1,0:T(8,128)(2,1)} %u_ref.1, bf16[6,128,256]{2,1,0:T(8,128)(2,1)} %bitcast.5, s32[6,128]{1,0:T(8,128)} %bitcast.7, f32[1,16]{1,0:T(1,128)} %bitcast.8, s32[2,32]{1,0:T(2,128)} %tb_in.1, s32[32,256]{1,0:T(8,128)} %bitcast.6), custom_call_target="tpu_custom_call" | custom-call | tf_op jit(solution)/shard_map/pallas_call | solution.py:640
  85.9 1.9 %shard_map.78 = (bf16[256,256]{1,0:T(8,128)(2,1)}, bf16[6,128,256]{2,1,0:T(8,128)(2,1)}) custom-call(bf16[256,256]{1,0:T(8,128)(2,1)} %get-tuple-element.6.u_ref, bf16[6,128,256]{2,1,0:T(8,128)(2,1)} %get-tuple-element.7.i_ref), custom_call_target="tpu_custom_call" | custom-call | tf_op jit(solution)/shard_map/pallas_call | solution.py:659

commit v6 on v5

--- a/solution.py
+++ b/solution.py
@@ -86,6 +86,19 @@
     def off(base, i, n):
         return lax.rem(base + i, n)
 
+    b0 = pl.multiple_of(r * BLK, BLK)
+    q0 = pl.multiple_of(y * QR, QR)
+    h0 = r * HB
+    own_items = pltpu.make_async_copy(it_ref, items.at[k0], l_sem.at[0])
+    own_items.start()
+    own_users = pltpu.make_async_copy(u_ref.at[pl.ds(b0, BLK)], ua.at[m], l_sem.at[1])
+    own_users.start()
+
+    small = [pltpu.make_async_copy(a, b, l_sem.at[2 + n]) for n, (a, b) in enumerate(
+        ((tb_in, tb_ref), (pos_in, pos_ref), (bk_in, bk_ref), (prop_in, prop_ref)))]
+    for copy in small:
+        copy.start()
+
     barrier = pltpu.get_barrier_semaphore()
 
     def greet(i, carry):
@@ -100,18 +113,6 @@
     pl.semaphore_signal(barrier, inc=1, device_id=sib, device_id_type=MESH)
     pl.semaphore_signal(barrier, inc=1, device_id=mate, device_id_type=MESH)
 
-    b0 = pl.multiple_of(r * BLK, BLK)
-    q0 = pl.multiple_of(y * QR, QR)
-    h0 = r * HB
-    own_items = pltpu.make_async_copy(it_ref, items.at[k0], l_sem.at[0])
-    own_items.start()
-    own_users = pltpu.make_async_copy(u_ref.at[pl.ds(b0, BLK)], ua.at[m], l_sem.at[1])
-    own_users.start()
-
-    small = [pltpu.make_async_copy(a, b, l_sem.at[2 + n]) for n, (a, b) in enumerate(
-        ((tb_in, tb_ref), (pos_in, pos_ref), (bk_in, bk_ref), (prop_in, prop_ref)))]
-    for copy in small:
-        copy.start()
     for copy in small:
         copy.wait()
 

time: 87.9 us -> 87.9 us (level)
  no operation moved by 1% of the time
where the time goes in v6:
time: 87.9 us; the launch traced here: 87.7 us
  Pallas kernels  87.1 us (99%)
    pallas_call x1, Pallas kernels, body(): pl.pallas_call(functools.partial(kernel, na), out_shape=(jax.ShapeDtypeSt...  85.2 us
    pallas_call x1, Pallas kernels, body(): pl.pallas_call(hand_over, out_shape=(jax.ShapeDtypeStruct(user_factors.sh...  1.87 us

profile of v6, /device:TPU:1, one launch (start us, length us, event | category | flops | bytes accessed | tf_op | source)
XLA Modules:
  0.0 87.7 jit_solution(14809599905032120141)
XLA Ops:
  0.6 85.2 %shard_map.77 = (bf16[256,256]{1,0:T(8,128)(2,1)}, bf16[6,128,256]{2,1,0:T(8,128)(2,1)}) custom-call(bf16[256,256]{1,0:T(8,128)(2,1)} %u_ref.1, bf16[6,128,256]{2,1,0:T(8,128)(2,1)} %bitcast.5, s32[6,128]{1,0:T(8,128)} %bitcast.7, f32[1,16]{1,0:T(1,128)} %bitcast.8, s32[2,32]{1,0:T(2,128)} %tb_in.1, s32[32,256]{1,0:T(8,128)} %bitcast.6), custom_call_target="tpu_custom_call" | custom-call | tf_op jit(solution)/shard_map/pallas_call | solution.py:641
  85.9 1.9 %shard_map.78 = (bf16[256,256]{1,0:T(8,128)(2,1)}, bf16[6,128,256]{2,1,0:T(8,128)(2,1)}) custom-call(bf16[256,256]{1,0:T(8,128)(2,1)} %get-tuple-element.6.u_ref, bf16[6,128,256]{2,1,0:T(8,128)(2,1)} %get-tuple-element.7.i_ref), custom_call_target="tpu_custom_call" | custom-call | tf_op jit(solution)/shard_map/pallas_call | solution.py:660
